TPU v7x, 32 devices: a whole 2x2x4 slice. The times are simulated.
32 devices in a mesh: gx: 4 (over y, x), gy: 4 (over z), mode: 2 (over core).
Axes of the slice: x: 2, y: 2, z: 4, core: 2. Of those that a mesh axis runs over, the one named last changes fastest.
Arguments:
- state: float32 [4, 64, 128, 1024], P(None, None, 'gx', ('gy', 'mode')), may hold values from -6 to 6
- depth_class: int32 [128, 1024], P('gx', ('gy', 'mode')), may hold values from 0 to 4
- vertical_inverse: float32 [4, 64, 64], replicated, as said below
- height: float32 [128, 1024], P('gx', ('gy', 'mode')), may hold values from -4 to 4
- transport: float32 [2, 128, 1024], P(None, 'gx', ('gy', 'mode')), may hold values from -4 to 4
Outputs:
- state_next: float32 [4, 64, 128, 1024], P(None, None, 'gx', ('gy', 'mode'))
- height_next: float32 [128, 1024], P('gx', ('gy', 'mode'))
- transport_next: float32 [2, 128, 1024], P(None, 'gx', ('gy', 'mode'))
Inputs may be any that keep to these rules, and one draw needn't show every extreme that they name: `depth_class`: 0 marks land; a column of class c has its top c * 16 levels active. `vertical_inverse`: entry c is used for columns of class c + 1 and acts on all 64 levels.
All inputs are finite; a program needn't handle non-finite values.
Results may differ from a plain program's by a relative error of at most 0.0003.
Values sent between devices are 32-bit elements; how exact they have to be, the bound alone decides.
A program may use at most 128 MiB of HBM per device.

v0:
```python
import jax
import jax.numpy as jnp
from jax import lax
from jax.sharding import PartitionSpec as P

SUB = 32


THERMAL = 0.8
HALINE = 0.6
PRESSURE_SCALE = 4.0
VISCOSITY = 0.1
STEP_TIME = 0.05
WAVE_STEP = 0.5
GRAVITY = 1.0
BOTTOM_DRAG = 0.05
CORIOLIS_BASE = 0.3
CORIOLIS_SLOPE = 0.4


def with_halo(cells, sides, width):
    for axis, dim in sides:
        count = lax.axis_size(axis)
        ends = count - 1
        head = lax.slice_in_dim(cells, 0, width, axis=dim)
        tail = lax.slice_in_dim(cells, cells.shape[dim] - width, cells.shape[dim], axis=dim)
        cells = jnp.concatenate(
            [
                lax.ppermute(tail, axis, [(i, (i + 1) % count) for i in range(ends)]),
                cells,
                lax.ppermute(head, axis, [((i + 1) % count, i) for i in range(ends)]),
            ],
            axis=dim,
        )
    return cells


def x_fourth(values):
    return (
        8.0 * (values[..., 3:-1, 2:-2] - values[..., 1:-3, 2:-2])
        - (values[..., 4:, 2:-2] - values[..., :-4, 2:-2])
    ) / 12.0


def y_fourth(values):
    return (
        8.0 * (values[..., 2:-2, 3:-1] - values[..., 2:-2, 1:-3])
        - (values[..., 2:-2, 4:] - values[..., 2:-2, :-4])
    ) / 12.0


def laplace(values):
    center = values[..., 2:-2, 2:-2]
    return (
        values[..., 3:-1, 2:-2]
        + values[..., 1:-3, 2:-2]
        + values[..., 2:-2, 3:-1]
        + values[..., 2:-2, 1:-3]
        - 4.0 * center
    )


def coriolis_row(anchor, number, total):
    position = (anchor + lax.broadcasted_iota(jnp.int32, (number,), 0)).astype(jnp.float32)
    return (CORIOLIS_BASE + CORIOLIS_SLOPE * (position + 0.5) / total)[None, :]


def baroclinic(state, padded, pressure, active, depth_class, inverse, coriolis):
    levels = state.shape[1]
    center = padded[:, :, 2:-2, 2:-2]
    east_vel = center[2]
    north_vel = center[3]
    tendency = -(east_vel * x_fourth(padded) + north_vel * y_fourth(padded)) + VISCOSITY * laplace(
        padded
    )
    zeros_field = jnp.zeros_like(east_vel)
    extra = jnp.stack(
        [
            zeros_field,
            zeros_field,
            -x_fourth(pressure) + coriolis * north_vel,
            -y_fourth(pressure) - coriolis * east_vel,
        ]
    )
    tendency = tendency + extra
    provisional = active * (center + STEP_TIME * tendency)
    solved = jnp.zeros_like(provisional)
    for class_index in range(inverse.shape[0]):
        chosen = (depth_class == class_index + 1).astype(jnp.float32)
        solved = solved + chosen * jnp.einsum(
            "kl,flxy->fkxy", inverse[class_index], provisional, precision=lax.Precision.HIGHEST
        )
    updated = active * solved + (1.0 - active) * state
    forcing = jnp.sum(active * tendency[2:4], axis=1) / levels
    return (updated, forcing)


def shrink(values):
    return values[..., 1:-1, 1:-1]


def x_slope(values):
    return (values[2:, 1:-1] - values[:-2, 1:-1]) * 0.5


def y_slope(values):
    return (values[1:-1, 2:] - values[1:-1, :-2]) * 0.5


def substep(moving, fixed_fields, coriolis):
    surface, east_flow, north_flow = (moving[0], moving[1], moving[2])
    column_depth = fixed_fields[2]
    sea_mask = (column_depth > 0.0).astype(jnp.float32)
    surface_mid = shrink(sea_mask) * (
        shrink(surface) - WAVE_STEP * (x_slope(east_flow) + y_slope(north_flow))
    )
    sea_inner = shrink(shrink(sea_mask))
    depth_inner = shrink(shrink(column_depth))
    force_east = shrink(shrink(fixed_fields[0]))
    force_north = shrink(shrink(fixed_fields[1]))
    coriolis_inner = coriolis[:, 2:-2]
    east_old = shrink(shrink(east_flow))
    north_old = shrink(shrink(north_flow))
    east_new = sea_inner * (
        east_old
        + WAVE_STEP
        * (
            -GRAVITY * depth_inner * x_slope(surface_mid)
            + coriolis_inner * north_old
            + force_east
            - BOTTOM_DRAG * east_old
        )
    )
    north_new = sea_inner * (
        north_old
        + WAVE_STEP
        * (
            -GRAVITY * depth_inner * y_slope(surface_mid)
            - coriolis_inner * east_new
            + force_north
            - BOTTOM_DRAG * north_old
        )
    )
    return jnp.stack([shrink(surface_mid), east_new, north_new])


def finish(updated, waves, active, depth_class, level_block, levels):
    counted = jnp.maximum(depth_class * level_block, 1).astype(jnp.float32)
    safe_depth = jnp.maximum(depth_class, 1).astype(jnp.float32) * level_block / levels
    column_means = jnp.sum(active * updated[2:4], axis=1) / counted
    carried = waves[1:3] / safe_depth
    velocity = updated[2:4] + active * (carried - column_means)[:, None]
    return jnp.concatenate([updated[0:2], velocity], axis=0)


def trim(values, margin):
    return values[..., margin : values.shape[-2] - margin, margin : values.shape[-1] - margin]


def advance(moving, fixed_wide, coriolis_wide, refresh, per_exchange, exchanges):

    def group(index, current):
        extended = refresh(current)
        for inner_step in range(per_exchange):
            margin = 2 * inner_step
            extended = substep(
                extended,
                trim(fixed_wide, margin),
                coriolis_wide[:, margin : coriolis_wide.shape[1] - margin],
            )
        return extended

    return lax.fori_loop(0, exchanges, group, moving)


def body(state, depth_class, vertical_inverse, height, transport):
    levels = state.shape[1]
    level_block = levels // vertical_inverse.shape[0]
    y_cells = depth_class.shape[1]
    level_ids = lax.broadcasted_iota(jnp.int32, (levels, 1, 1), 0)
    active = (level_ids < depth_class[None] * level_block).astype(jnp.float32)
    masked = state * active[None]
    padded = with_halo(masked, (("gx", 2), (("gy", "mode"), 3)), 2)
    column_blocks = lax.axis_size(("gy", "mode"))
    anchor = lax.axis_index(("gy", "mode")) * y_cells
    coriolis = coriolis_row(anchor, y_cells, y_cells * column_blocks)[0]
    density = -THERMAL * padded[0] + HALINE * padded[1]
    row_ids = lax.broadcasted_iota(jnp.int32, (levels, levels), 0)
    col_ids = lax.broadcasted_iota(jnp.int32, (levels, levels), 1)
    lower_ones = (row_ids >= col_ids).astype(jnp.float32)
    pressure = (
        PRESSURE_SCALE
        / levels
        * jnp.einsum("kl,lxy->kxy", lower_ones, density, precision=lax.Precision.HIGHEST)
    )
    updated, forcing = baroclinic(
        state, padded, pressure, active, depth_class, vertical_inverse, coriolis
    )
    column_depth = depth_class.astype(jnp.float32) * level_block / levels
    sea_mask = (depth_class > 0).astype(jnp.float32)
    moving = jnp.stack([height, transport[0], transport[1]]) * sea_mask
    fixed_fields = jnp.stack([forcing[0], forcing[1], column_depth])
    per_exchange = 4
    depth_rim = 2 * per_exchange
    exchanges = SUB // per_exchange
    fixed_wide = with_halo(fixed_fields, (("gx", 1), (("gy", "mode"), 2)), depth_rim)
    coriolis_wide = coriolis_row(
        anchor - depth_rim, y_cells + 2 * depth_rim, y_cells * column_blocks
    )

    def refresh_block(current):
        return with_halo(current, (("gx", 1), (("gy", "mode"), 2)), depth_rim)

    waves = advance(moving, fixed_wide, coriolis_wide, refresh_block, per_exchange, exchanges)
    state_next = finish(updated, waves, active, depth_class, level_block, levels)
    return (state_next, waves[0], waves[1:3])


def solution(mesh):
    placed = (
        P(None, None, "gx", ("gy", "mode")),
        P("gx", ("gy", "mode")),
        P(),
        P("gx", ("gy", "mode")),
        P(None, "gx", ("gy", "mode")),
    )
    return jax.shard_map(
        body,
        mesh=mesh,
        in_specs=placed,
        out_specs=(
            P(None, None, "gx", ("gy", "mode")),
            P("gx", ("gy", "mode")),
            P(None, "gx", ("gy", "mode")),
        ),
        check_vma=False,
    )
```

profile of v0, /device:TPU:1, one launch (start us, length us, event | category | flops | bytes accessed | tf_op | source)
XLA Modules:
  0.0 271.5 jit_solution(1439750469455536824)
XLA Ops:
  1.5 4.6 %copy_multiply_fusion = f32[4,64,32,128]{3,1,2,0:T(8,128)S(1)} fusion(f32[4,64,32,128]{3,2,1,0:T(8,128)} %param.7, f32[64,32,128]{2,0,1:T(8,128)S(1)} %fusion.118), kind=kLoop, calls=%fused_computation.158 | loop fusion | flops 1048576 | bytes 9437184 | tf_op jit(solution)/shard_map/mul | solution.py:182
  9.5 4.6 %collective-permute-start.5 = (f32[4,64,2,128]{3,1,2,0:T(8,128)S(1)}, f32[4,64,2,128]{3,1,2,0:T(8,128)S(1)}, u32[]{:S(2)}, u32[]{:S(2)}) collective-permute-start(f32[4,64,2,128]{3,1,2,0:T(8,128)S(1)} %get-tuple-element.131), channel_id=1, source_target_pairs={{0,8},{8,16},{16,24},{1,9},{9,17},{17,25},{2,10},{10,18},{18,26},{... | collective-permute-start | bytes 786440 | tf_op jit(solution)/shard_map/ppermute | solution.py:29
  21.7 5.2 %fusion.144 = (f32[4,64,36,2]{3,1,2,0:T(8,128)}, f32[4,64,36,2]{3,1,2,0:T(8,128)}) fusion(f32[4,64,36,128]{3,1,2,0:T(8,128)S(1)} %pad_maximum_fusion.2), kind=kLoop, calls=%fused_computation.244 | loop fusion | bytes 294912 | tf_op jit(solution)/shard_map/slice | solution.py:26
  26.9 3.2 %copy.12 = f32[4,64,36,2]{1,0,3,2:T(4,128)S(1)} copy(f32[4,64,36,2]{3,1,2,0:T(8,128)} %get-tuple-element.124) | data formatting | bytes 147456 | tf_op jit(solution)/shard_map/slice | solution.py:25
  30.1 3.5 %collective-permute-start.6 = (f32[4,64,36,2]{1,0,3,2:T(4,128)S(1)}, f32[4,64,36,2]{1,0,3,2:T(4,128)S(1)}, u32[]{:S(2)}, u32[]{:S(2)}) collective-permute-start(f32[4,64,36,2]{1,0,3,2:T(4,128)S(1)} %copy.12), channel_id=1, source_target_pairs={{1,0},{2,1},{3,2},{4,3},{5,4},{6,5},{7,6},{9,8},{10,9},{11,10},{12... | collective-permute-start | bytes 221192 | tf_op jit(solution)/shard_map/ppermute | solution.py:31
  33.6 3.2 %copy.14 = f32[4,64,36,2]{1,0,3,2:T(4,128)S(1)} copy(f32[4,64,36,2]{3,1,2,0:T(8,128)} %get-tuple-element.123) | data formatting | bytes 147456 | tf_op jit(solution)/shard_map/slice | solution.py:26
  36.8 3.5 %collective-permute-start.7 = (f32[4,64,36,2]{1,0,3,2:T(4,128)S(1)}, f32[4,64,36,2]{1,0,3,2:T(4,128)S(1)}, u32[]{:S(2)}, u32[]{:S(2)}) collective-permute-start(f32[4,64,36,2]{1,0,3,2:T(4,128)S(1)} %copy.14), channel_id=1, source_target_pairs={{0,1},{1,2},{2,3},{3,4},{4,5},{5,6},{6,7},{8,9},{9,10},{10,11},{11... | collective-permute-start | bytes 221192 | tf_op jit(solution)/shard_map/ppermute | solution.py:29
  40.4 3.0 %copy.13 = f32[4,64,36,2]{3,1,2,0:T(8,128)} copy(f32[4,64,36,2]{1,0,3,2:T(4,128)S(1)} %collective-permute-done.6) | data formatting | bytes 147456 | tf_op jit(solution)/shard_map/ppermute | solution.py:31
  43.4 3.0 %copy.15 = f32[4,64,36,2]{3,1,2,0:T(8,128)} copy(f32[4,64,36,2]{1,0,3,2:T(4,128)S(1)} %collective-permute-done.7) | data formatting | bytes 147456 | tf_op jit(solution)/shard_map/ppermute | solution.py:29
  46.4 6.8 %fusion.101 = f32[64,36,132]{2,0,1:T(8,128)S(1)} fusion(f32[4,64,36,2]{3,1,2,0:T(8,128)} %copy.13, f32[4,64,36,2]{3,1,2,0:T(8,128)} %copy.15, f32[4,64,2,128]{3,1,2,0:T(8,128)S(1)} %collective-permute-done.4, f32[4,64,32,128]{3,1,2,0:T(8,128)} %copy-done, f32[4,64,2,128]{3,1,2,0:T(8,128)} %copy-done.5), kind=kOutput, calls=%fused_computation.181 | convolution fusion | flops 237223936 | bytes 6082560 | tf_op jit(solution)/shard_map/kl,lxy->kxy/dot_general | solution.py:194
  53.2 3.9 %fusion.119 = (f32[64,32,128]{2,0,1:T(8,128)}, f32[64,32,128]{2,0,1:T(8,128)}, f32[1,64,32,128]{3,1,2,0:T(8,128)}, f32[1,64,32,128]{3,1,2,0:T(8,128)}) fusion(f32[4,64,32,128]{3,1,2,0:T(8,128)S(1)} %copy-done.1, f32[128]{0:T(128)S(1)} %multiply_add_fusion.2, f32[64,36,132]{2,0,1:T(8,128)S(1)} %fusion.101), kind=kLoop, calls=%fused_computation.204 | loop fusion | flops 4718592 | bytes 14680576 | tf_op jit(solution)/shard_map/mul | solution.py:73
  57.1 12.7 %add_multiply_fusion = (f32[4,64,32,128]{3,1,2,0:T(8,128)S(1)}, f32[4,64,32,128]{3,1,2,0:T(8,128)}) fusion(f32[64,32,128]{2,0,1:T(8,128)S(1)} %fusion.118, f32[4,64,32,128]{3,2,1,0:T(8,128)} %param.7, f32[1,64,32,128]{3,1,2,0:T(8,128)} %get-tuple-element.129, f32[1,64,32,128]{3,1,2,0:T(8,128)} %get-tuple-element.130, f32[4]{0:T(128)} %pad.22.clone, ...), kind=kLoop, calls=%fused_computation.157 | loop fusion | flops 44040192 | bytes 22691856 | tf_op jit(solution)/shard_map/mul | solution.py:86
  69.8 4.0 %fusion.122 = f32[4,32,128,64]{2,3,1,0:T(8,128)S(1)} fusion(f32[4,64,32,128]{3,1,2,0:T(8,128)S(1)} %get-tuple-element.99, f32[4,64,64]{2,1,0:T(8,128)S(1)} %copy-done.7), kind=kOutput, calls=%fused_computation.211 | convolution fusion | flops 805306368 | bytes 8421376 | tf_op jit(solution)/shard_map/kl,flxy->fkxy/dot_general | solution.py:90
  73.8 5.6 %fusion.124 = f32[4,32,128,64]{2,3,1,0:T(8,128)} fusion(f32[4,64,32,128]{3,1,2,0:T(8,128)S(1)} %get-tuple-element.99, f32[4,64,64]{2,1,0:T(8,128)S(1)} %copy-done.7), kind=kOutput, calls=%fused_computation.213 | convolution fusion | flops 805306368 | bytes 8421376 | tf_op jit(solution)/shard_map/kl,flxy->fkxy/dot_general | solution.py:90
  79.4 5.4 %fusion.126 = f32[4,32,128,64]{2,3,1,0:T(8,128)} fusion(f32[4,64,32,128]{3,1,2,0:T(8,128)S(1)} %get-tuple-element.99, f32[4,64,64]{2,1,0:T(8,128)S(1)} %copy-done.7), kind=kOutput, calls=%fused_computation.215 | convolution fusion | flops 805306368 | bytes 8421376 | tf_op jit(solution)/shard_map/kl,flxy->fkxy/dot_general | solution.py:90
  84.8 10.2 %fusion.85 = f32[4,64,32,128]{3,1,2,0:T(8,128)S(1)} fusion(f32[4,32,128,64]{2,3,1,0:T(8,128)S(1)} %fusion.122, f32[4,32,128,64]{2,3,1,0:T(8,128)} %fusion.124, f32[4,32,128,64]{2,3,1,0:T(8,128)} %fusion.126, f32[4,64,32,128]{3,2,1,0:T(8,128)S(1)} %copy-done.2, f32[4,64,32,128]{3,1,2,0:T(8,128)S(1)} %get-tuple-element.99, f32[64,32,128]{2,0,1:T(8,128)S(1)} %copy-done.4, ...), kind=kOutput, calls=%fused_computation.156 | convolution fusion | flops 815792128 | bytes 27361280 | tf_op jit(solution)/shard_map/kl,flxy->fkxy/dot_general | solution.py:90
  99.5 5.6 %collective-permute-start.8 = (f32[3,8,128]{2,1,0:T(8,128)S(1)}, f32[3,8,128]{2,1,0:T(8,128)S(1)}, u32[]{:S(2)}, u32[]{:S(2)}) collective-permute-start(f32[3,8,128]{2,1,0:T(8,128)S(1)} %get-tuple-element.135), channel_id=1, source_target_pairs={{0,8},{8,16},{16,24},{1,9},{9,17},{17,25},{2,10},{10,18},{18,26},{... | collective-permute-start | bytes 36872 | tf_op jit(solution)/shard_map/ppermute | solution.py:29
  106.4 4.7 %collective-permute-done.9 = f32[3,8,128]{2,1,0:T(8,128)S(1)} collective-permute-done((f32[3,8,128]{2,1,0:T(8,128)S(1)}, f32[3,8,128]{2,1,0:T(8,128)S(1)}, u32[]{:S(2)}, u32[]{:S(2)}) %collective-permute-start.9) | collective-permute-done | bytes 12320 | tf_op jit(solution)/shard_map/ppermute | solution.py:31
  111.3 4.4 %collective-permute-start.10 = (f32[3,48,8]{2,1,0:T(8,128)S(1)}, f32[3,48,8]{2,1,0:T(8,128)S(1)}, u32[]{:S(2)}, u32[]{:S(2)}) collective-permute-start(f32[3,48,8]{2,1,0:T(8,128)S(1)} %get-tuple-element.133), channel_id=1, source_target_pairs={{0,1},{1,2},{2,3},{3,4},{4,5},{5,6},{6,7},{8,9},{9,10},{10,11},{11... | collective-permute-start | bytes 13832 | tf_op jit(solution)/shard_map/ppermute | solution.py:29
  117.6 3.7 %collective-permute-done.11 = f32[3,48,8]{2,1,0:T(8,128)S(1)} collective-permute-done((f32[3,48,8]{2,1,0:T(8,128)S(1)}, f32[3,48,8]{2,1,0:T(8,128)S(1)}, u32[]{:S(2)}, u32[]{:S(2)}) %collective-permute-start.11) | collective-permute-done | bytes 4640 | tf_op jit(solution)/shard_map/ppermute | solution.py:31
  121.5 140.9 %while.13 = (s32[]{:T(128)}, f32[3,32,128]{2,1,0:T(8,128)S(1)}, f32[3,48,144]{2,1,0:T(8,128)S(1)}, f32[1,144]{1,0:T(1,128)S(1)}, s32[]{:T(128)}) while((s32[]{:T(128)}, f32[3,32,128]{2,1,0:T(8,128)S(1)}, f32[3,48,144]{2,1,0:T(8,128)S(1)}, f32[1,144]{1,0:T(1,128)S(1)}, s32[]{:T(128)}) %tuple.92), condition=%wide.region_2.0_spmd, body=%wide.region_1.0_spmd.sunk | while | flops 713922 | bytes 3157181 | solution.py:173
  121.7 4.5 %collective-permute-start = (f32[3,8,128]{2,1,0:T(8,128)S(1)}, f32[3,8,128]{2,1,0:T(8,128)S(1)}, u32[]{:S(2)}, u32[]{:S(2)}) collective-permute-start(f32[3,8,128]{2,1,0:T(8,128)S(1)} %get-tuple-element.203), channel_id=1, source_target_pairs={{0,8},{8,16},{16,24},{1,9},{9,17},{17,25},{2,10},{10,18},{18,26},{... | collective-permute-start | bytes 36872 | tf_op jit(solution)/shard_map/while/body/eval_jaxpr/ppermute | solution.py:29
  132.7 3.6 %collective-permute-start.3 = (f32[3,48,8]{2,1,0:T(8,128)S(1)}, f32[3,48,8]{2,1,0:T(8,128)S(1)}, u32[]{:S(2)}, u32[]{:S(2)}) collective-permute-start(f32[3,48,8]{2,1,0:T(8,128)S(1)} %get-tuple-element.206), channel_id=1, source_target_pairs={{0,1},{1,2},{2,3},{3,4},{4,5},{5,6},{6,7},{8,9},{9,10},{10,11},{11... | collective-permute-start | bytes 13832 | tf_op jit(solution)/shard_map/while/body/eval_jaxpr/ppermute | solution.py:29
  139.2 3.1 %collective-permute-start = (f32[3,8,128]{2,1,0:T(8,128)S(1)}, f32[3,8,128]{2,1,0:T(8,128)S(1)}, u32[]{:S(2)}, u32[]{:S(2)}) collective-permute-start(f32[3,8,128]{2,1,0:T(8,128)S(1)} %get-tuple-element.203), channel_id=1, source_target_pairs={{0,8},{8,16},{16,24},{1,9},{9,17},{17,25},{2,10},{10,18},{18,26},{... | collective-permute-start | bytes 36872 | tf_op jit(solution)/shard_map/while/body/eval_jaxpr/ppermute | solution.py:29
  148.8 5.7 %collective-permute-start.3 = (f32[3,48,8]{2,1,0:T(8,128)S(1)}, f32[3,48,8]{2,1,0:T(8,128)S(1)}, u32[]{:S(2)}, u32[]{:S(2)}) collective-permute-start(f32[3,48,8]{2,1,0:T(8,128)S(1)} %get-tuple-element.206), channel_id=1, source_target_pairs={{0,1},{1,2},{2,3},{3,4},{4,5},{5,6},{6,7},{8,9},{9,10},{10,11},{11... | collective-permute-start | bytes 13832 | tf_op jit(solution)/shard_map/while/body/eval_jaxpr/ppermute | solution.py:29
  166.3 5.7 %collective-permute-start.3 = (f32[3,48,8]{2,1,0:T(8,128)S(1)}, f32[3,48,8]{2,1,0:T(8,128)S(1)}, u32[]{:S(2)}, u32[]{:S(2)}) collective-permute-start(f32[3,48,8]{2,1,0:T(8,128)S(1)} %get-tuple-element.206), channel_id=1, source_target_pairs={{0,1},{1,2},{2,3},{3,4},{4,5},{5,6},{6,7},{8,9},{9,10},{10,11},{11... | collective-permute-start | bytes 13832 | tf_op jit(solution)/shard_map/while/body/eval_jaxpr/ppermute | solution.py:29
  183.8 5.7 %collective-permute-start.3 = (f32[3,48,8]{2,1,0:T(8,128)S(1)}, f32[3,48,8]{2,1,0:T(8,128)S(1)}, u32[]{:S(2)}, u32[]{:S(2)}) collective-permute-start(f32[3,48,8]{2,1,0:T(8,128)S(1)} %get-tuple-element.206), channel_id=1, source_target_pairs={{0,1},{1,2},{2,3},{3,4},{4,5},{5,6},{6,7},{8,9},{9,10},{10,11},{11... | collective-permute-start | bytes 13832 | tf_op jit(solution)/shard_map/while/body/eval_jaxpr/ppermute | solution.py:29
  201.3 5.7 %collective-permute-start.3 = (f32[3,48,8]{2,1,0:T(8,128)S(1)}, f32[3,48,8]{2,1,0:T(8,128)S(1)}, u32[]{:S(2)}, u32[]{:S(2)}) collective-permute-start(f32[3,48,8]{2,1,0:T(8,128)S(1)} %get-tuple-element.206), channel_id=1, source_target_pairs={{0,1},{1,2},{2,3},{3,4},{4,5},{5,6},{6,7},{8,9},{9,10},{10,11},{11... | collective-permute-start | bytes 13832 | tf_op jit(solution)/shard_map/while/body/eval_jaxpr/ppermute | solution.py:29
  218.8 5.7 %collective-permute-start.3 = (f32[3,48,8]{2,1,0:T(8,128)S(1)}, f32[3,48,8]{2,1,0:T(8,128)S(1)}, u32[]{:S(2)}, u32[]{:S(2)}) collective-permute-start(f32[3,48,8]{2,1,0:T(8,128)S(1)} %get-tuple-element.206), channel_id=1, source_target_pairs={{0,1},{1,2},{2,3},{3,4},{4,5},{5,6},{6,7},{8,9},{9,10},{10,11},{11... | collective-permute-start | bytes 13832 | tf_op jit(solution)/shard_map/while/body/eval_jaxpr/ppermute | solution.py:29
  236.4 5.7 %collective-permute-start.3 = (f32[3,48,8]{2,1,0:T(8,128)S(1)}, f32[3,48,8]{2,1,0:T(8,128)S(1)}, u32[]{:S(2)}, u32[]{:S(2)}) collective-permute-start(f32[3,48,8]{2,1,0:T(8,128)S(1)} %get-tuple-element.206), channel_id=1, source_target_pairs={{0,1},{1,2},{2,3},{3,4},{4,5},{5,6},{6,7},{8,9},{9,10},{10,11},{11... | collective-permute-start | bytes 13832 | tf_op jit(solution)/shard_map/while/body/eval_jaxpr/ppermute | solution.py:29
  253.9 5.7 %collective-permute-start.3 = (f32[3,48,8]{2,1,0:T(8,128)S(1)}, f32[3,48,8]{2,1,0:T(8,128)S(1)}, u32[]{:S(2)}, u32[]{:S(2)}) collective-permute-start(f32[3,48,8]{2,1,0:T(8,128)S(1)} %get-tuple-element.206), channel_id=1, source_target_pairs={{0,1},{1,2},{2,3},{3,4},{4,5},{5,6},{6,7},{8,9},{9,10},{10,11},{11... | collective-permute-start | bytes 13832 | tf_op jit(solution)/shard_map/while/body/eval_jaxpr/ppermute | solution.py:29
  267.1 4.4 %copy.19 = f32[4,64,32,128]{3,2,1,0:T(8,128)} copy(f32[4,64,32,128]{3,1,2,0:T(8,128)S(1)} %pad_maximum_fusion.13) | data formatting | bytes 8388608
  (336 shorter events, 111.9 us)
Async XLA Ops:
  8.2 10.0 %collective-permute-start.4 = (f32[4,64,2,128]{3,1,2,0:T(8,128)S(1)}, f32[4,64,2,128]{3,1,2,0:T(8,128)S(1)}, u32[]{:S(2)}, u32[]{:S(2)}) collective-permute-start(f32[4,64,2,128]{3,1,2,0:T(8,128)S(1)} %get-tuple-element.132), channel_id=1, source_target_pairs={{8,0},{16,8},{24,16},{9,1},{17,9},{25,17},{10,2},{18,10},{26,18},{... | collective-permute-start | bytes 786440 | tf_op jit(solution)/shard_map/ppermute | solution.py:31
  9.5 9.5 %collective-permute-start.5 = (f32[4,64,2,128]{3,1,2,0:T(8,128)S(1)}, f32[4,64,2,128]{3,1,2,0:T(8,128)S(1)}, u32[]{:S(2)}, u32[]{:S(2)}) collective-permute-start(f32[4,64,2,128]{3,1,2,0:T(8,128)S(1)} %get-tuple-element.131), channel_id=1, source_target_pairs={{0,8},{8,16},{16,24},{1,9},{9,17},{17,25},{2,10},{10,18},{18,26},{... | collective-permute-start | bytes 786440 | tf_op jit(solution)/shard_map/ppermute | solution.py:29
  30.1 10.2 %collective-permute-start.6 = (f32[4,64,36,2]{1,0,3,2:T(4,128)S(1)}, f32[4,64,36,2]{1,0,3,2:T(4,128)S(1)}, u32[]{:S(2)}, u32[]{:S(2)}) collective-permute-start(f32[4,64,36,2]{1,0,3,2:T(4,128)S(1)} %copy.12), channel_id=1, source_target_pairs={{1,0},{2,1},{3,2},{4,3},{5,4},{6,5},{7,6},{9,8},{10,9},{11,10},{12... | collective-permute-start | bytes 221192 | tf_op jit(solution)/shard_map/ppermute | solution.py:31
  36.8 6.6 %collective-permute-start.7 = (f32[4,64,36,2]{1,0,3,2:T(4,128)S(1)}, f32[4,64,36,2]{1,0,3,2:T(4,128)S(1)}, u32[]{:S(2)}, u32[]{:S(2)}) collective-permute-start(f32[4,64,36,2]{1,0,3,2:T(4,128)S(1)} %copy.14), channel_id=1, source_target_pairs={{0,1},{1,2},{2,3},{3,4},{4,5},{5,6},{6,7},{8,9},{9,10},{10,11},{11... | collective-permute-start | bytes 221192 | tf_op jit(solution)/shard_map/ppermute | solution.py:29
  99.5 7.0 %collective-permute-start.8 = (f32[3,8,128]{2,1,0:T(8,128)S(1)}, f32[3,8,128]{2,1,0:T(8,128)S(1)}, u32[]{:S(2)}, u32[]{:S(2)}) collective-permute-start(f32[3,8,128]{2,1,0:T(8,128)S(1)} %get-tuple-element.135), channel_id=1, source_target_pairs={{0,8},{8,16},{16,24},{1,9},{9,17},{17,25},{2,10},{10,18},{18,26},{... | collective-permute-start | bytes 36872 | tf_op jit(solution)/shard_map/ppermute | solution.py:29
  105.1 6.1 %collective-permute-start.9 = (f32[3,8,128]{2,1,0:T(8,128)S(1)}, f32[3,8,128]{2,1,0:T(8,128)S(1)}, u32[]{:S(2)}, u32[]{:S(2)}) collective-permute-start(f32[3,8,128]{2,1,0:T(8,128)S(1)} %get-tuple-element.136), channel_id=1, source_target_pairs={{8,0},{16,8},{24,16},{9,1},{17,9},{25,17},{10,2},{18,10},{26,18},{... | collective-permute-start | bytes 36872 | tf_op jit(solution)/shard_map/ppermute | solution.py:31
  111.3 6.3 %collective-permute-start.10 = (f32[3,48,8]{2,1,0:T(8,128)S(1)}, f32[3,48,8]{2,1,0:T(8,128)S(1)}, u32[]{:S(2)}, u32[]{:S(2)}) collective-permute-start(f32[3,48,8]{2,1,0:T(8,128)S(1)} %get-tuple-element.133), channel_id=1, source_target_pairs={{0,1},{1,2},{2,3},{3,4},{4,5},{5,6},{6,7},{8,9},{9,10},{10,11},{11... | collective-permute-start | bytes 13832 | tf_op jit(solution)/shard_map/ppermute | solution.py:29
  115.7 5.7 %collective-permute-start.11 = (f32[3,48,8]{2,1,0:T(8,128)S(1)}, f32[3,48,8]{2,1,0:T(8,128)S(1)}, u32[]{:S(2)}, u32[]{:S(2)}) collective-permute-start(f32[3,48,8]{2,1,0:T(8,128)S(1)} %get-tuple-element.134), channel_id=1, source_target_pairs={{1,0},{2,1},{3,2},{4,3},{5,4},{6,5},{7,6},{9,8},{10,9},{11,10},{12... | collective-permute-start | bytes 13832 | tf_op jit(solution)/shard_map/ppermute | solution.py:31
  121.7 6.5 %collective-permute-start = (f32[3,8,128]{2,1,0:T(8,128)S(1)}, f32[3,8,128]{2,1,0:T(8,128)S(1)}, u32[]{:S(2)}, u32[]{:S(2)}) collective-permute-start(f32[3,8,128]{2,1,0:T(8,128)S(1)} %get-tuple-element.203), channel_id=1, source_target_pairs={{0,8},{8,16},{16,24},{1,9},{9,17},{17,25},{2,10},{10,18},{18,26},{... | collective-permute-start | bytes 36872 | tf_op jit(solution)/shard_map/while/body/eval_jaxpr/ppermute | solution.py:29
  130.8 5.9 %collective-permute-start.2 = (f32[3,48,8]{2,1,0:T(8,128)S(1)}, f32[3,48,8]{2,1,0:T(8,128)S(1)}, u32[]{:S(2)}, u32[]{:S(2)}) collective-permute-start(f32[3,48,8]{2,1,0:T(8,128)S(1)} %get-tuple-element.205), channel_id=1, source_target_pairs={{1,0},{2,1},{3,2},{4,3},{5,4},{6,5},{7,6},{9,8},{10,9},{11,10},{12... | collective-permute-start | bytes 13832 | tf_op jit(solution)/shard_map/while/body/eval_jaxpr/ppermute | solution.py:31
  132.7 5.0 %collective-permute-start.3 = (f32[3,48,8]{2,1,0:T(8,128)S(1)}, f32[3,48,8]{2,1,0:T(8,128)S(1)}, u32[]{:S(2)}, u32[]{:S(2)}) collective-permute-start(f32[3,48,8]{2,1,0:T(8,128)S(1)} %get-tuple-element.206), channel_id=1, source_target_pairs={{0,1},{1,2},{2,3},{3,4},{4,5},{5,6},{6,7},{8,9},{9,10},{10,11},{11... | collective-permute-start | bytes 13832 | tf_op jit(solution)/shard_map/while/body/eval_jaxpr/ppermute | solution.py:29
  139.2 5.1 %collective-permute-start = (f32[3,8,128]{2,1,0:T(8,128)S(1)}, f32[3,8,128]{2,1,0:T(8,128)S(1)}, u32[]{:S(2)}, u32[]{:S(2)}) collective-permute-start(f32[3,8,128]{2,1,0:T(8,128)S(1)} %get-tuple-element.203), channel_id=1, source_target_pairs={{0,8},{8,16},{16,24},{1,9},{9,17},{17,25},{2,10},{10,18},{18,26},{... | collective-permute-start | bytes 36872 | tf_op jit(solution)/shard_map/while/body/eval_jaxpr/ppermute | solution.py:29
  146.9 7.9 %collective-permute-start.2 = (f32[3,48,8]{2,1,0:T(8,128)S(1)}, f32[3,48,8]{2,1,0:T(8,128)S(1)}, u32[]{:S(2)}, u32[]{:S(2)}) collective-permute-start(f32[3,48,8]{2,1,0:T(8,128)S(1)} %get-tuple-element.205), channel_id=1, source_target_pairs={{1,0},{2,1},{3,2},{4,3},{5,4},{6,5},{7,6},{9,8},{10,9},{11,10},{12... | collective-permute-start | bytes 13832 | tf_op jit(solution)/shard_map/while/body/eval_jaxpr/ppermute | solution.py:31
  148.8 7.1 %collective-permute-start.3 = (f32[3,48,8]{2,1,0:T(8,128)S(1)}, f32[3,48,8]{2,1,0:T(8,128)S(1)}, u32[]{:S(2)}, u32[]{:S(2)}) collective-permute-start(f32[3,48,8]{2,1,0:T(8,128)S(1)} %get-tuple-element.206), channel_id=1, source_target_pairs={{0,1},{1,2},{2,3},{3,4},{4,5},{5,6},{6,7},{8,9},{9,10},{10,11},{11... | collective-permute-start | bytes 13832 | tf_op jit(solution)/shard_map/while/body/eval_jaxpr/ppermute | solution.py:29
  157.3 4.5 %collective-permute-start = (f32[3,8,128]{2,1,0:T(8,128)S(1)}, f32[3,8,128]{2,1,0:T(8,128)S(1)}, u32[]{:S(2)}, u32[]{:S(2)}) collective-permute-start(f32[3,8,128]{2,1,0:T(8,128)S(1)} %get-tuple-element.203), channel_id=1, source_target_pairs={{0,8},{8,16},{16,24},{1,9},{9,17},{17,25},{2,10},{10,18},{18,26},{... | collective-permute-start | bytes 36872 | tf_op jit(solution)/shard_map/while/body/eval_jaxpr/ppermute | solution.py:29
  164.4 7.9 %collective-permute-start.2 = (f32[3,48,8]{2,1,0:T(8,128)S(1)}, f32[3,48,8]{2,1,0:T(8,128)S(1)}, u32[]{:S(2)}, u32[]{:S(2)}) collective-permute-start(f32[3,48,8]{2,1,0:T(8,128)S(1)} %get-tuple-element.205), channel_id=1, source_target_pairs={{1,0},{2,1},{3,2},{4,3},{5,4},{6,5},{7,6},{9,8},{10,9},{11,10},{12... | collective-permute-start | bytes 13832 | tf_op jit(solution)/shard_map/while/body/eval_jaxpr/ppermute | solution.py:31
  166.3 7.1 %collective-permute-start.3 = (f32[3,48,8]{2,1,0:T(8,128)S(1)}, f32[3,48,8]{2,1,0:T(8,128)S(1)}, u32[]{:S(2)}, u32[]{:S(2)}) collective-permute-start(f32[3,48,8]{2,1,0:T(8,128)S(1)} %get-tuple-element.206), channel_id=1, source_target_pairs={{0,1},{1,2},{2,3},{3,4},{4,5},{5,6},{6,7},{8,9},{9,10},{10,11},{11... | collective-permute-start | bytes 13832 | tf_op jit(solution)/shard_map/while/body/eval_jaxpr/ppermute | solution.py:29
  174.8 4.5 %collective-permute-start = (f32[3,8,128]{2,1,0:T(8,128)S(1)}, f32[3,8,128]{2,1,0:T(8,128)S(1)}, u32[]{:S(2)}, u32[]{:S(2)}) collective-permute-start(f32[3,8,128]{2,1,0:T(8,128)S(1)} %get-tuple-element.203), channel_id=1, source_target_pairs={{0,8},{8,16},{16,24},{1,9},{9,17},{17,25},{2,10},{10,18},{18,26},{... | collective-permute-start | bytes 36872 | tf_op jit(solution)/shard_map/while/body/eval_jaxpr/ppermute | solution.py:29
  181.9 7.9 %collective-permute-start.2 = (f32[3,48,8]{2,1,0:T(8,128)S(1)}, f32[3,48,8]{2,1,0:T(8,128)S(1)}, u32[]{:S(2)}, u32[]{:S(2)}) collective-permute-start(f32[3,48,8]{2,1,0:T(8,128)S(1)} %get-tuple-element.205), channel_id=1, source_target_pairs={{1,0},{2,1},{3,2},{4,3},{5,4},{6,5},{7,6},{9,8},{10,9},{11,10},{12... | collective-permute-start | bytes 13832 | tf_op jit(solution)/shard_map/while/body/eval_jaxpr/ppermute | solution.py:31
  183.8 7.1 %collective-permute-start.3 = (f32[3,48,8]{2,1,0:T(8,128)S(1)}, f32[3,48,8]{2,1,0:T(8,128)S(1)}, u32[]{:S(2)}, u32[]{:S(2)}) collective-permute-start(f32[3,48,8]{2,1,0:T(8,128)S(1)} %get-tuple-element.206), channel_id=1, source_target_pairs={{0,1},{1,2},{2,3},{3,4},{4,5},{5,6},{6,7},{8,9},{9,10},{10,11},{11... | collective-permute-start | bytes 13832 | tf_op jit(solution)/shard_map/while/body/eval_jaxpr/ppermute | solution.py:29
  192.3 4.5 %collective-permute-start = (f32[3,8,128]{2,1,0:T(8,128)S(1)}, f32[3,8,128]{2,1,0:T(8,128)S(1)}, u32[]{:S(2)}, u32[]{:S(2)}) collective-permute-start(f32[3,8,128]{2,1,0:T(8,128)S(1)} %get-tuple-element.203), channel_id=1, source_target_pairs={{0,8},{8,16},{16,24},{1,9},{9,17},{17,25},{2,10},{10,18},{18,26},{... | collective-permute-start | bytes 36872 | tf_op jit(solution)/shard_map/while/body/eval_jaxpr/ppermute | solution.py:29
  199.4 7.9 %collective-permute-start.2 = (f32[3,48,8]{2,1,0:T(8,128)S(1)}, f32[3,48,8]{2,1,0:T(8,128)S(1)}, u32[]{:S(2)}, u32[]{:S(2)}) collective-permute-start(f32[3,48,8]{2,1,0:T(8,128)S(1)} %get-tuple-element.205), channel_id=1, source_target_pairs={{1,0},{2,1},{3,2},{4,3},{5,4},{6,5},{7,6},{9,8},{10,9},{11,10},{12... | collective-permute-start | bytes 13832 | tf_op jit(solution)/shard_map/while/body/eval_jaxpr/ppermute | solution.py:31
  201.3 7.1 %collective-permute-start.3 = (f32[3,48,8]{2,1,0:T(8,128)S(1)}, f32[3,48,8]{2,1,0:T(8,128)S(1)}, u32[]{:S(2)}, u32[]{:S(2)}) collective-permute-start(f32[3,48,8]{2,1,0:T(8,128)S(1)} %get-tuple-element.206), channel_id=1, source_target_pairs={{0,1},{1,2},{2,3},{3,4},{4,5},{5,6},{6,7},{8,9},{9,10},{10,11},{11... | collective-permute-start | bytes 13832 | tf_op jit(solution)/shard_map/while/body/eval_jaxpr/ppermute | solution.py:29
  209.9 4.5 %collective-permute-start = (f32[3,8,128]{2,1,0:T(8,128)S(1)}, f32[3,8,128]{2,1,0:T(8,128)S(1)}, u32[]{:S(2)}, u32[]{:S(2)}) collective-permute-start(f32[3,8,128]{2,1,0:T(8,128)S(1)} %get-tuple-element.203), channel_id=1, source_target_pairs={{0,8},{8,16},{16,24},{1,9},{9,17},{17,25},{2,10},{10,18},{18,26},{... | collective-permute-start | bytes 36872 | tf_op jit(solution)/shard_map/while/body/eval_jaxpr/ppermute | solution.py:29
  216.9 7.9 %collective-permute-start.2 = (f32[3,48,8]{2,1,0:T(8,128)S(1)}, f32[3,48,8]{2,1,0:T(8,128)S(1)}, u32[]{:S(2)}, u32[]{:S(2)}) collective-permute-start(f32[3,48,8]{2,1,0:T(8,128)S(1)} %get-tuple-element.205), channel_id=1, source_target_pairs={{1,0},{2,1},{3,2},{4,3},{5,4},{6,5},{7,6},{9,8},{10,9},{11,10},{12... | collective-permute-start | bytes 13832 | tf_op jit(solution)/shard_map/while/body/eval_jaxpr/ppermute | solution.py:31
  218.8 7.1 %collective-permute-start.3 = (f32[3,48,8]{2,1,0:T(8,128)S(1)}, f32[3,48,8]{2,1,0:T(8,128)S(1)}, u32[]{:S(2)}, u32[]{:S(2)}) collective-permute-start(f32[3,48,8]{2,1,0:T(8,128)S(1)} %get-tuple-element.206), channel_id=1, source_target_pairs={{0,1},{1,2},{2,3},{3,4},{4,5},{5,6},{6,7},{8,9},{9,10},{10,11},{11... | collective-permute-start | bytes 13832 | tf_op jit(solution)/shard_map/while/body/eval_jaxpr/ppermute | solution.py:29
  227.4 4.5 %collective-permute-start = (f32[3,8,128]{2,1,0:T(8,128)S(1)}, f32[3,8,128]{2,1,0:T(8,128)S(1)}, u32[]{:S(2)}, u32[]{:S(2)}) collective-permute-start(f32[3,8,128]{2,1,0:T(8,128)S(1)} %get-tuple-element.203), channel_id=1, source_target_pairs={{0,8},{8,16},{16,24},{1,9},{9,17},{17,25},{2,10},{10,18},{18,26},{... | collective-permute-start | bytes 36872 | tf_op jit(solution)/shard_map/while/body/eval_jaxpr/ppermute | solution.py:29
  234.4 7.9 %collective-permute-start.2 = (f32[3,48,8]{2,1,0:T(8,128)S(1)}, f32[3,48,8]{2,1,0:T(8,128)S(1)}, u32[]{:S(2)}, u32[]{:S(2)}) collective-permute-start(f32[3,48,8]{2,1,0:T(8,128)S(1)} %get-tuple-element.205), channel_id=1, source_target_pairs={{1,0},{2,1},{3,2},{4,3},{5,4},{6,5},{7,6},{9,8},{10,9},{11,10},{12... | collective-permute-start | bytes 13832 | tf_op jit(solution)/shard_map/while/body/eval_jaxpr/ppermute | solution.py:31
  236.4 7.1 %collective-permute-start.3 = (f32[3,48,8]{2,1,0:T(8,128)S(1)}, f32[3,48,8]{2,1,0:T(8,128)S(1)}, u32[]{:S(2)}, u32[]{:S(2)}) collective-permute-start(f32[3,48,8]{2,1,0:T(8,128)S(1)} %get-tuple-element.206), channel_id=1, source_target_pairs={{0,1},{1,2},{2,3},{3,4},{4,5},{5,6},{6,7},{8,9},{9,10},{10,11},{11... | collective-permute-start | bytes 13832 | tf_op jit(solution)/shard_map/while/body/eval_jaxpr/ppermute | solution.py:29
  244.9 4.5 %collective-permute-start = (f32[3,8,128]{2,1,0:T(8,128)S(1)}, f32[3,8,128]{2,1,0:T(8,128)S(1)}, u32[]{:S(2)}, u32[]{:S(2)}) collective-permute-start(f32[3,8,128]{2,1,0:T(8,128)S(1)} %get-tuple-element.203), channel_id=1, source_target_pairs={{0,8},{8,16},{16,24},{1,9},{9,17},{17,25},{2,10},{10,18},{18,26},{... | collective-permute-start | bytes 36872 | tf_op jit(solution)/shard_map/while/body/eval_jaxpr/ppermute | solution.py:29
  251.9 7.9 %collective-permute-start.2 = (f32[3,48,8]{2,1,0:T(8,128)S(1)}, f32[3,48,8]{2,1,0:T(8,128)S(1)}, u32[]{:S(2)}, u32[]{:S(2)}) collective-permute-start(f32[3,48,8]{2,1,0:T(8,128)S(1)} %get-tuple-element.205), channel_id=1, source_target_pairs={{1,0},{2,1},{3,2},{4,3},{5,4},{6,5},{7,6},{9,8},{10,9},{11,10},{12... | collective-permute-start | bytes 13832 | tf_op jit(solution)/shard_map/while/body/eval_jaxpr/ppermute | solution.py:31
  253.9 7.1 %collective-permute-start.3 = (f32[3,48,8]{2,1,0:T(8,128)S(1)}, f32[3,48,8]{2,1,0:T(8,128)S(1)}, u32[]{:S(2)}, u32[]{:S(2)}) collective-permute-start(f32[3,48,8]{2,1,0:T(8,128)S(1)} %get-tuple-element.206), channel_id=1, source_target_pairs={{0,1},{1,2},{2,3},{3,4},{4,5},{5,6},{6,7},{8,9},{9,10},{10,11},{11... | collective-permute-start | bytes 13832 | tf_op jit(solution)/shard_map/while/body/eval_jaxpr/ppermute | solution.py:29
  (21 other events, 137.7 us)
where the time goes:
time: 273 us; the launch traced here: 272 us
  starting transfers between devices  118 us (43%)
  other arithmetic  45.4 us (17%)
  waiting for transfers between devices  39.9 us (15%)
  local copies, waits for them, and re-layouts  32.9 us (12%)
  matrix products  32 us (12%)
    ppermute x20, starting transfers between devices, with_halo(): lax.ppermute(tail, axis, [(i, (i + 1) % count) for i in range(ends)])  84.6 us
    ppermute x20, starting transfers between devices, with_halo(): lax.ppermute(head, axis, [((i + 1) % count, i) for i in range(ends)])  33.6 us
    ppermute x20, waiting for transfers between devices, with_halo(): lax.ppermute(head, axis, [((i + 1) % count, i) for i in range(ends)])  30.2 us
    dot_general x4, matrix products, baroclinic(): jnp.einsum('kl,flxy->fkxy', inverse[class_index], provisional, precision=...  25.2 us
    mul x1, other arithmetic, baroclinic(): provisional = active * (center + STEP_TIME * tendency)  12.7 us
    ppermute x20, waiting for transfers between devices, with_halo(): lax.ppermute(tail, axis, [(i, (i + 1) % count) for i in range(ends)])  9.64 us
    slice x12, local copies, waits for them, and re-layouts, with_halo(): lax.slice_in_dim(cells, cells.shape[dim] - width, cells.shape[dim], axis=...  9.19 us
    unnamed x27, local copies, waits for them, and re-layouts  8.44 us
  transfers between devices with their start and end apart: 40, of which 20 were waited for; matrix products, arithmetic and copies ran while one was open for 6% of the time, Pallas kernels for 0%

commit v1 on v0

v1 whole, which is shorter than its diff:
```python
import functools

import jax
import jax.numpy as jnp
from jax import lax
from jax.experimental import pallas as pl
from jax.experimental.pallas import tpu as pltpu
from jax.sharding import PartitionSpec as P

SUB = 32
THERMAL = 0.8
HALINE = 0.6
PRESSURE_SCALE = 4.0
VISCOSITY = 0.1
STEP_TIME = 0.05
BOTTOM_DRAG = 0.05
CORIOLIS_BASE = 0.3
CORIOLIS_SLOPE = 0.4
MESH = pl.DeviceIdType.MESH
OFFSETS = [(dx, dy) for dx in (1, -1, 2, -2, 0) for dy in (0, 1, -1) if (dx, dy) != (0, 0)]


def step_kernel(
    gxn, gyn, mdn,
    state_hbm, cls_ref, inv_ref, height_ref, transport_ref,
    upd_hbm, waves_ref, corr_ref,
    raw, mq, prov, updv, packed, from_left, from_right,
    win, fwin, wl, fo, flow, cons, nat, mean,
    raw_sem, out_sem, x_send, x_recv, y_send, y_recv, w_send, w_recv, f_send, f_recv,
):
    levels = inv_ref.shape[1]
    classes = inv_ref.shape[0]
    block = levels // classes
    rows = cls_ref.shape[0]
    cols = cls_ref.shape[1]
    span = win.shape[2]
    strips = span // 8
    blocks = span // rows
    gx = lax.axis_index("gx")
    yy = lax.axis_index("gy") * mdn + lax.axis_index("mode")
    yn = gyn * mdn
    ny = cols * yn

    def slot_of(dx):
        return (gx + dx) if blocks == gxn else (dx + 2)

    def inside(dx, dy):
        return (gx + dx >= 0) & (gx + dx < gxn) & (yy + dy >= 0) & (yy + dy < yn)

    def device(dx, dy):
        y2 = yy + dy
        return (gx + dx, y2 // mdn, lax.rem(y2, mdn))

    offsets = [o for o in OFFSETS if abs(o[0]) < gxn and abs(o[1]) < yn]

    loads = [pltpu.make_async_copy(state_hbm.at[f], raw.at[f], raw_sem.at[f]) for f in range(4)]
    for c in loads:
        c.start()

    win[...] = jnp.zeros_like(win)
    fwin[...] = jnp.zeros_like(fwin)
    cls = cls_ref[...]
    sea = (cls > 0).astype(jnp.float32)

    def own(ref):
        return ref.at[:, pl.ds(pl.multiple_of(slot_of(0) * rows, rows), rows), :]

    mine = own(win.at[0])
    mine[0] = cls.astype(jnp.float32)
    mine[1] = sea * height_ref[...]
    mine[2] = sea * transport_ref[0]
    mine[3] = sea * transport_ref[1]

    @pl.when(gx == 0)
    def _():
        mq[:, 0:2] = jnp.zeros((4, 2, levels, cols), jnp.float32)

    @pl.when(gx == gxn - 1)
    def _():
        mq[:, rows + 2 : rows + 4] = jnp.zeros((4, 2, levels, cols), jnp.float32)

    @pl.when(yy == 0)
    def _():
        from_left[...] = jnp.zeros_like(from_left)

    @pl.when(yy == yn - 1)
    def _():
        from_right[...] = jnp.zeros_like(from_right)

    barrier = pltpu.get_barrier_semaphore()
    total = 0
    for dx, dy in offsets:
        ok = inside(dx, dy)
        total = total + ok.astype(jnp.int32)

        @pl.when(ok)
        def _(dx=dx, dy=dy):
            pl.semaphore_signal(barrier, inc=1, device_id=device(dx, dy), device_id_type=MESH)

    pl.semaphore_wait(barrier, total)
    for c in loads:
        c.wait()

    level_block = lax.broadcasted_iota(jnp.int32, (levels, cols), 0) // block
    lane_full = lax.broadcasted_iota(jnp.int32, (levels, cols), 1)
    lane = lax.broadcasted_iota(jnp.int32, (8, cols), 1)
    sub = lax.broadcasted_iota(jnp.int32, (8, cols), 0)

    def mask_column(x):
        act = level_block < cls_ref[pl.ds(x, 1), :]
        spot = (lane_full >= 4 * x) & (lane_full < 4 * x + 4)
        shift = lax.rem(4 * x + 2, cols)
        for f in range(4):
            v = jnp.where(act, raw[f, pl.ds(x, levels, stride=rows), :], 0.0)
            mq[f, x + 2] = v
            packed[f] = jnp.where(spot, pltpu.roll(v, shift, 1), packed[f])

    packed[...] = jnp.zeros_like(packed)

    def edge_columns(work):
        def at(e, carry):
            work(jnp.where(e < 2, e, rows - 4 + e))
            return carry

        lax.fori_loop(0, 4, at, 0)

    def inner_columns(work):
        def at(x, carry):
            work(x)
            return carry

        lax.fori_loop(2, rows - 2, at, 0)

    edge_columns(mask_column)

    def x_copy(way):
        src, dst = (mq.at[:, 2:4], mq.at[:, rows + 2 : rows + 4]) if way < 0 else (
            mq.at[:, rows : rows + 2], mq.at[:, 0:2])
        i = 0 if way < 0 else 1
        return pltpu.make_async_remote_copy(
            src_ref=src, dst_ref=dst, send_sem=x_send.at[i], recv_sem=x_recv.at[i],
            device_id=device(way, 0), device_id_type=MESH)

    def y_copy(way):
        dst = from_right if way < 0 else from_left
        i = 0 if way < 0 else 1
        return pltpu.make_async_remote_copy(
            src_ref=packed, dst_ref=dst, send_sem=y_send.at[i], recv_sem=y_recv.at[i],
            device_id=device(0, way), device_id_type=MESH)

    def window_copy(ref, k, send, recv, arriving):
        dx, dy = offsets[k]
        side = {0: 0, 1: 1, -1: 2}[dy]
        if arriving:
            slot = slot_of(-dx)
        elif blocks == gxn:
            slot = gx
        else:
            slot = 2 - dx
        dst = ref.at[side, :, pl.ds(pl.multiple_of(slot * rows, rows), rows), :]
        return pltpu.make_async_remote_copy(
            src_ref=own(ref.at[0]), dst_ref=dst, send_sem=send.at[k], recv_sem=recv.at[k],
            device_id=device(-dx, -dy) if arriving else device(dx, dy), device_id_type=MESH)

    for way in (-1, 1):
        @pl.when(inside(way, 0))
        def _(way=way):
            x_copy(way).start()

    inner_columns(mask_column)
    for way in (-1, 1):
        @pl.when(inside(0, way))
        def _(way=way):
            y_copy(way).start()

    for k, (dx, dy) in enumerate(offsets):
        @pl.when(inside(dx, dy))
        def _(k=k):
            window_copy(win, k, w_send, w_recv, False).start()

    start = 0
    for c in range(classes):
        part = inv_ref[c][: block * (c + 1), :]
        high = part.astype(jnp.bfloat16)
        low = (part - high.astype(jnp.float32)).astype(jnp.bfloat16)
        wl[start : start + block * (c + 1), :] = jnp.concatenate([high, high, low], axis=1)
        start += block * (c + 1)

    for way in (-1, 1):
        @pl.when(inside(0, -way))
        def _(way=way):
            y_copy(way).wait_recv()

    slot_left = lax.rem(lane, 4) < 2
    position = (yy * cols + lane).astype(jnp.float32)
    coriolis = CORIOLIS_BASE + CORIOLIS_SLOPE * (position + 0.5) / ny

    def tendency_column(x):
        cls_row = cls_ref[pl.ds(x, 1), :]
        shift = lax.rem(2 * cols - 2 - 4 * x, cols)
        sum_east = jnp.zeros((8, cols), jnp.float32)
        sum_north = jnp.zeros((8, cols), jnp.float32)
        carry_x = jnp.zeros((1, cols), jnp.float32)
        carry_y = jnp.zeros((1, cols), jnp.float32)
        for l0 in range(0, levels, 8):
            act = jnp.broadcast_to((cls_row > l0 // block).astype(jnp.float32), (8, cols))
            u = mq[2, x + 2, l0 : l0 + 8, :]
            v = mq[3, x + 2, l0 : l0 + 8, :]
            u12 = u * (1.0 / 12.0)
            v12 = v * (1.0 / 12.0)
            density_x = density_y = None
            for f in range(4):
                c = mq[f, x + 2, l0 : l0 + 8, :]
                xm1 = mq[f, x + 1, l0 : l0 + 8, :]
                xp1 = mq[f, x + 3, l0 : l0 + 8, :]
                xm2 = mq[f, x, l0 : l0 + 8, :]
                xp2 = mq[f, x + 4, l0 : l0 + 8, :]
                h = jnp.where(slot_left, from_left[f, l0 : l0 + 8, :], from_right[f, l0 : l0 + 8, :])
                h = pltpu.roll(h, shift, 1)
                yp1 = pltpu.roll(jnp.where(lane < 1, h, c), cols - 1, 1)
                yp2 = pltpu.roll(jnp.where(lane < 2, h, c), cols - 2, 1)
                ym1 = pltpu.roll(jnp.where(lane > cols - 2, h, c), 1, 1)
                ym2 = pltpu.roll(jnp.where(lane > cols - 3, h, c), 2, 1)
                x12 = 8.0 * (xp1 - xm1) - (xp2 - xm2)
                y12 = 8.0 * (yp1 - ym1) - (yp2 - ym2)
                lap = (xp1 + xm1) + (yp1 + ym1) - 4.0 * c
                t = VISCOSITY * lap - (u12 * x12 + v12 * y12)
                if f == 0:
                    density_x, density_y = -THERMAL * x12, -THERMAL * y12
                elif f == 1:
                    gx_, gy_ = density_x + HALINE * x12, density_y + HALINE * y12
                    for k in (1, 2, 4):
                        gx_ = gx_ + jnp.where(sub >= k, pltpu.roll(gx_, k, 0), 0.0)
                        gy_ = gy_ + jnp.where(sub >= k, pltpu.roll(gy_, k, 0), 0.0)
                    gx_ = gx_ + carry_x
                    gy_ = gy_ + carry_y
                    carry_x, carry_y = gx_[7:8, :], gy_[7:8, :]
                elif f == 2:
                    t = t - (PRESSURE_SCALE / levels / 12.0) * gx_ + coriolis * v
                    sum_east = sum_east + act * t
                else:
                    t = t - (PRESSURE_SCALE / levels / 12.0) * gy_ - coriolis * u
                    sum_north = sum_north + act * t
                prov[x, f, l0 : l0 + 8, :] = act * (c + STEP_TIME * t)
        fo[0, pl.ds(x, 1), :] = jnp.sum(sum_east, axis=0, keepdims=True) * (1.0 / levels)
        fo[1, pl.ds(x, 1), :] = jnp.sum(sum_north, axis=0, keepdims=True) * (1.0 / levels)

    inner_columns(tendency_column)
    for way in (-1, 1):
        @pl.when(inside(-way, 0))
        def _(way=way):
            x_copy(way).wait_recv()

    edge_columns(tendency_column)

    mine_f = own(fwin.at[0])
    mine_f[0] = fo[0]
    mine_f[1] = fo[1]
    for k, (dx, dy) in enumerate(offsets):
        @pl.when(inside(dx, dy))
        def _(k=k):
            window_copy(fwin, k, f_send, f_recv, False).start()

    starts = [block * c * (c + 1) // 2 for c in range(classes)]

    def solve_column(x, carry):
        cls_row = cls_ref[pl.ds(x, 1), :]
        for pair in (0, 2):
            p = jnp.concatenate([prov[x, pair], prov[x, pair + 1]], axis=1)
            high = p.astype(jnp.bfloat16)
            low = (p - high.astype(jnp.float32)).astype(jnp.bfloat16)
            o = jnp.dot(
                wl[...], jnp.concatenate([high, low, high], axis=0),
                preferred_element_type=jnp.float32)
            for g in range(2):
                f = pair + g
                total_f = jnp.zeros((block, cols), jnp.float32)
                for b in range(classes):
                    picked = None
                    for c in range(b, classes):
                        r = starts[c] + block * b
                        piece = o[r : r + block, g * cols : (g + 1) * cols]
                        picked = piece if picked is None else jnp.where(cls_row == c + 1, piece, picked)
                    where = pl.ds(x + block * b * rows, block, stride=rows)
                    updv[f, where, :] = jnp.where(cls_row > b, picked, raw[f, where, :])
                    total_f = total_f + jnp.where(cls_row > b, picked, 0.0)
                if f >= 2:
                    mean[f - 2, pl.ds(x, 1), :] = jnp.sum(total_f, axis=0, keepdims=True)
        return carry

    lax.fori_loop(0, rows, solve_column, 0)
    stores = [pltpu.make_async_copy(updv.at[f], upd_hbm.at[f], out_sem.at[f]) for f in range(4)]
    for c in stores:
        c.start()

    for k, (dx, dy) in enumerate(offsets):
        @pl.when(inside(-dx, -dy))
        def _(k=k):
            window_copy(win, k, w_send, w_recv, True).wait_recv()
            window_copy(fwin, k, f_send, f_recv, True).wait_recv()

    half = lane < cols // 2
    place = [yy * cols + lane, yy * cols + jnp.where(half, lane + cols, lane - cols)]
    turn = [0.5 * (CORIOLIS_BASE + CORIOLIS_SLOPE * (p.astype(jnp.float32) + 0.5) / ny) for p in place]

    def strip(ref, i, j):
        at = pl.ds(i, 8, stride=strips)
        a = ref[0, j, at, :]
        return a, jnp.where(half, ref[2, j, at, :], ref[1, j, at, :])

    for i in range(strips):
        c = strip(win, i, 0)
        fields = [strip(win, i, 1 + j) for j in range(3)]
        f0, f1 = strip(fwin, i, 0), strip(fwin, i, 1)
        for t in range(2):
            wet = (c[t] > 0.0).astype(jnp.float32)
            cons[0, t, i] = 0.25 * wet
            cons[1, t, i] = c[t] * (0.25 * block / levels)
            cons[2, t, i] = 0.5 * wet * f0[t]
            cons[3, t, i] = 0.5 * wet * f1[t]
            for j in range(3):
                flow[j, t, i + 1] = fields[j][t]

    def edges(j):
        for t in range(2):
            flow[j, t, 0] = jnp.where(sub >= 1, pltpu.roll(flow[j, t, strips], 1, 0), 0.0)
            flow[j, t, strips + 1] = jnp.where(sub < 7, pltpu.roll(flow[j, t, 1], 7, 0), 0.0)

    first, last = lane == 0, lane == cols - 1

    def y_difference(a, b):
        ap, bp = pltpu.roll(a, cols - 1, 1), pltpu.roll(b, cols - 1, 1)
        am, bm = pltpu.roll(a, 1, 1), pltpu.roll(b, 1, 1)
        return (
            jnp.where(last, bp, ap) - jnp.where(first, bm, am),
            jnp.where(last, ap, bp) - jnp.where(first, am, bm),
        )

    edges(1)
    keep = 1.0 - 0.5 * BOTTOM_DRAG

    def substep(step, carry):
        for i in range(1, strips + 1):
            dy = y_difference(flow[2, 0, i], flow[2, 1, i])
            for t in range(2):
                dx = flow[1, t, i + 1] - flow[1, t, i - 1]
                flow[0, t, i] = flow[0, t, i] - cons[0, t, i - 1] * (dx + dy[t])
        edges(0)
        for i in range(1, strips + 1):
            dy = y_difference(flow[0, 0, i], flow[0, 1, i])
            for t in range(2):
                dx = flow[0, t, i + 1] - flow[0, t, i - 1]
                east, north, depth = flow[1, t, i], flow[2, t, i], cons[1, t, i - 1]
                east = (keep * east + turn[t] * north) + (cons[2, t, i - 1] - depth * dx)
                flow[1, t, i] = east
                flow[2, t, i] = (keep * north - turn[t] * east) + (cons[3, t, i - 1] - depth * dy[t])
        edges(1)
        return carry

    lax.fori_loop(0, SUB, substep, 0)

    for j in range(3):
        for i in range(strips):
            nat[j, pl.ds(i, 8, stride=strips), :] = flow[j, 0, i + 1]
    final = own(nat)
    for j in range(3):
        waves_ref[j] = final[j]
    counted = jnp.maximum(cls * block, 1).astype(jnp.float32)
    depth = jnp.maximum(cls, 1).astype(jnp.float32) * block / levels
    for j in range(2):
        corr_ref[j] = final[1 + j] / depth - mean[j] / counted

    for c in stores:
        c.wait()
    for way in (-1, 1):
        @pl.when(inside(way, 0))
        def _(way=way):
            x_copy(way).wait_send()

        @pl.when(inside(0, way))
        def _(way=way):
            y_copy(way).wait_send()
    for k, (dx, dy) in enumerate(offsets):
        @pl.when(inside(dx, dy))
        def _(k=k):
            window_copy(win, k, w_send, w_recv, False).wait_send()
            window_copy(fwin, k, f_send, f_recv, False).wait_send()


def finish_kernel(block, upd_ref, cls_ref, corr_ref, out_ref):
    cls = cls_ref[...]
    depth = pl.program_id(0)
    rows = cls.shape[0]
    out_ref[0:2] = upd_ref[0:2]
    for j in range(2):
        add = jnp.where(cls > depth, corr_ref[j], 0.0)
        for k in range(block):
            out_ref[2 + j, k * rows : (k + 1) * rows] = upd_ref[2 + j, k * rows : (k + 1) * rows] + add


def body(gxn, gyn, mdn, state, depth_class, vertical_inverse, height, transport):
    _, levels, rows, cols = state.shape
    classes = vertical_inverse.shape[0]
    block = levels // classes
    span = rows * min(5, gxn)
    strips = span // 8
    f32 = jnp.float32
    vmem = pl.BlockSpec(memory_space=pltpu.VMEM)
    hbm = pl.BlockSpec(memory_space=pl.ANY)
    k = len(OFFSETS)
    dma = pltpu.SemaphoreType.DMA
    wide = block * classes * (classes + 1) // 2
    flat = state.reshape(4, levels * rows, cols)
    upd, waves, corr = pl.pallas_call(
        functools.partial(step_kernel, gxn, gyn, mdn),
        out_shape=(
            jax.ShapeDtypeStruct(flat.shape, f32),
            jax.ShapeDtypeStruct((3, rows, cols), f32),
            jax.ShapeDtypeStruct((2, rows, cols), f32),
        ),
        in_specs=[hbm, vmem, vmem, vmem, vmem],
        out_specs=(hbm, vmem, vmem),
        scratch_shapes=[
            pltpu.VMEM((4, levels * rows, cols), f32),
            pltpu.VMEM((4, rows + 4, levels, cols), f32),
            pltpu.VMEM((rows, 4, levels, cols), f32),
            pltpu.VMEM((4, levels * rows, cols), f32),
            pltpu.VMEM((4, levels, cols), f32),
            pltpu.VMEM((4, levels, cols), f32),
            pltpu.VMEM((4, levels, cols), f32),
            pltpu.VMEM((3, 4, span, cols), f32),
            pltpu.VMEM((3, 2, span, cols), f32),
            pltpu.VMEM((wide, 3 * levels), jnp.bfloat16),
            pltpu.VMEM((2, rows, cols), f32),
            pltpu.VMEM((3, 2, strips + 2, 8, cols), f32),
            pltpu.VMEM((4, 2, strips, 8, cols), f32),
            pltpu.VMEM((3, span, cols), f32),
            pltpu.VMEM((2, rows, cols), f32),
            dma((4,)), dma((4,)), dma((2,)), dma((2,)), dma((2,)), dma((2,)),
            dma((k,)), dma((k,)), dma((k,)), dma((k,)),
        ],
        compiler_params=pltpu.CompilerParams(
            collective_id=0, has_side_effects=True, vmem_limit_bytes=48 * 2**20),
        cost_estimate=pl.CostEstimate(flops=10**9, bytes_accessed=2**23, transcendentals=0),
    )(flat, depth_class, vertical_inverse, height, transport)
    out = pl.pallas_call(
        functools.partial(finish_kernel, block),
        grid=(classes,),
        out_shape=jax.ShapeDtypeStruct(flat.shape, f32),
        in_specs=[
            pl.BlockSpec((4, block * rows, cols), lambda i: (0, i, 0)),
            pl.BlockSpec((rows, cols), lambda i: (0, 0)),
            pl.BlockSpec((2, rows, cols), lambda i: (0, 0, 0)),
        ],
        out_specs=pl.BlockSpec((4, block * rows, cols), lambda i: (0, i, 0)),
        compiler_params=pltpu.CompilerParams(vmem_limit_bytes=24 * 2**20),
        cost_estimate=pl.CostEstimate(flops=2**20, bytes_accessed=2**23, transcendentals=0),
    )(upd, depth_class, corr)
    return out.reshape(state.shape), waves[0], waves[1:3]


def solution(mesh):
    placed = (
        P(None, None, "gx", ("gy", "mode")),
        P("gx", ("gy", "mode")),
        P(),
        P("gx", ("gy", "mode")),
        P(None, "gx", ("gy", "mode")),
    )
    sizes = mesh.shape
    return jax.shard_map(
        functools.partial(body, sizes["gx"], sizes["gy"], sizes["mode"]),
        mesh=mesh,
        in_specs=placed,
        out_specs=(
            P(None, None, "gx", ("gy", "mode")),
            P("gx", ("gy", "mode")),
            P(None, "gx", ("gy", "mode")),
        ),
        check_vma=False,
    )
```

time: 273 us -> 54.7 us (0.20)
  starting transfers between devices: 118 us -> 0 us
  Pallas kernels: 0 us -> 49.4 us
  other arithmetic: 45.4 us -> 0 us
  waiting for transfers between devices: 39.9 us -> 0 us
  matrix products: 32 us -> 0 us
  local copies, waits for them, and re-layouts: 32.9 us -> 4.31 us
    ppermute x40 -> x0, starting transfers between devices: 118 us -> none  [the longest x20 84.6 us: with_halo(): lax.ppermute(tail, axis, [(i, (i + 1) % count) for i in range(ends)])]
    pallas_call x0 -> x2, Pallas kernels: none -> 49.4 us  [the longest x1 46.7 us: body(): pl.pallas_call(functools.partial(step_kernel, gxn, gyn, mdn), out_shape=(...]
    ppermute x40 -> x0, waiting for transfers between devices: 39.9 us -> none  [the longest x20 30.2 us: with_halo(): lax.ppermute(head, axis, [((i + 1) % count, i) for i in range(ends)])]
    dot_general x5 -> x0, matrix products: 32 us -> none  [the longest x4 25.2 us: baroclinic(): jnp.einsum('kl,flxy->fkxy', inverse[class_index], provisional, precision=...]
    mul x60 -> x0, other arithmetic: 29.6 us -> none  [the longest x1 12.7 us: baroclinic(): provisional = active * (center + STEP_TIME * tendency)]
    slice x45 -> x1, local copies, waits for them, and re-layouts: 14.2 us -> 0.62 us  [body(): return (out.reshape(state.shape), waves[0], waves[1:3])]
    ppermute x2 -> x0, local copies, waits for them, and re-layouts: 6 us -> none  [the longest x1 3.04 us: with_halo(): lax.ppermute(head, axis, [((i + 1) % count, i) for i in range(ends)])]
    unnamed x27 -> x8, local copies, waits for them, and re-layouts: 8.44 us -> 3.09 us
  transfers between devices with their start and end apart: 40 -> 0, of which waited for: 20 -> 0; matrix products, arithmetic and copies ran while one was open for 6% -> 0% of each run, Pallas kernels for 0% -> 0%
where the time goes in v1:
time: 54.7 us; the launch traced here: 54.4 us
  Pallas kernels  49.4 us (90%)
  local copies, waits for them, and re-layouts  4.31 us (8%)
  between operations  0.65 us (1%)
    pallas_call x1, Pallas kernels, body(): pl.pallas_call(functools.partial(step_kernel, gxn, gyn, mdn), out_shape=(...  46.7 us
    unnamed x8, local copies, waits for them, and re-layouts  3.09 us
    pallas_call x1, Pallas kernels, body(): pl.pallas_call(functools.partial(finish_kernel, block), grid=(classes,),...  2.67 us

profile of v1, /device:TPU:1, one launch (start us, length us, event | category | flops | bytes accessed | tf_op | source)
XLA Modules:
  0.0 54.4 jit_solution(1127269633016495144)
XLA Ops:
  0.6 0.0 copy-start
  0.6 0.9 %copy-done = f32[4,64,64]{2,1,0:T(8,128)S(1)} copy-done((f32[4,64,64]{2,1,0:T(8,128)S(1)}, f32[4,64,64]{2,1,0:T(8,128)}, u32[]{:S(2)}) %copy-start) | copy-done | bytes 65560
  1.5 0.0 copy-start.1
  1.5 0.7 %copy-done.1 = s32[32,128]{1,0:T(8,128)S(1)} copy-done((s32[32,128]{1,0:T(8,128)S(1)}, s32[32,128]{1,0:T(8,128)}, u32[]{:S(2)}) %copy-start.1) | copy-done | bytes 16408
  2.3 0.0 copy-start.2
  2.3 0.8 %copy-done.2 = f32[2,32,128]{2,1,0:T(8,128)S(1)} copy-done((f32[2,32,128]{2,1,0:T(8,128)S(1)}, f32[2,32,128]{2,1,0:T(8,128)}, u32[]{:S(2)}) %copy-start.2) | copy-done | bytes 32792
  3.0 0.0 copy-start.3
  3.0 0.7 %copy-done.3 = f32[32,128]{1,0:T(8,128)S(1)} copy-done((f32[32,128]{1,0:T(8,128)S(1)}, f32[32,128]{1,0:T(8,128)}, u32[]{:S(2)}) %copy-start.3) | copy-done | bytes 16408
  3.7 46.7 %shard_map.76 = (f32[4,2048,128]{2,1,0:T(8,128)S(1)}, f32[3,32,128]{2,1,0:T(8,128)S(1)}, f32[2,32,128]{2,1,0:T(8,128)S(1)}) custom-call(f32[4,2048,128]{2,1,0:T(8,128)} %bitcast.4, s32[32,128]{1,0:T(8,128)S(1)} %copy-done.1, f32[4,64,64]{2,1,0:T(8,128)S(1)} %copy-done, f32[32,128]{1,0:T(8,128)S(1)} %copy-done.3, f32[2,32,128]{2,1,0:T(8,128)S(1)} %copy-done.2), custom_call_target="tpu_custom_call" | custom-call | flops 1000000000 | bytes 8388608 | tf_op jit(solution)/shard_map/pallas_call | solution.py:414
  50.5 2.7 %shard_map.77 = f32[4,2048,128]{2,1,0:T(8,128)} custom-call(f32[4,2048,128]{2,1,0:T(8,128)S(1)} %get-tuple-element.6.upd_ref, s32[32,128]{1,0:T(8,128)S(1)} %copy-done.1, f32[2,32,128]{2,1,0:T(8,128)S(1)} %get-tuple-element.7.corr_ref), custom_call_target="tpu_custom_call" | custom-call | flops 1048576 | bytes 8388608 | tf_op jit(solution)/shard_map/pallas_call | solution.py:446
  53.1 0.6 %slice_bitcast_fusion = f32[32,128]{1,0:T(8,128)} fusion(f32[3,32,128]{2,1,0:T(8,128)S(1)} %get-tuple-element.8), kind=kLoop, calls=%fused_computation | loop fusion | bytes 32768 | tf_op jit(solution)/shard_map/squeeze | solution.py:459
  53.7 0.6 %slice.7 = f32[2,32,128]{2,1,0:T(8,128)} slice(f32[3,32,128]{2,1,0:T(8,128)S(1)} %get-tuple-element.8), slice={[1:3], [0:32], [0:128]} | slice | bytes 65536 | tf_op jit(solution)/shard_map/slice | solution.py:459
Async XLA Ops:
  0.6 0.9 %copy-start = (f32[4,64,64]{2,1,0:T(8,128)S(1)}, f32[4,64,64]{2,1,0:T(8,128)}, u32[]{:S(2)}) copy-start(f32[4,64,64]{2,1,0:T(8,128)} %inv_ref.1) | copy-start | bytes 196612
  1.5 0.7 %copy-start.1 = (s32[32,128]{1,0:T(8,128)S(1)}, s32[32,128]{1,0:T(8,128)}, u32[]{:S(2)}) copy-start(s32[32,128]{1,0:T(8,128)} %cls_ref.3) | copy-start | bytes 49156
  2.3 0.8 %copy-start.2 = (f32[2,32,128]{2,1,0:T(8,128)S(1)}, f32[2,32,128]{2,1,0:T(8,128)}, u32[]{:S(2)}) copy-start(f32[2,32,128]{2,1,0:T(8,128)} %transport_ref.1) | copy-start | bytes 98308
  3.0 0.7 %copy-start.3 = (f32[32,128]{1,0:T(8,128)S(1)}, f32[32,128]{1,0:T(8,128)}, u32[]{:S(2)}) copy-start(f32[32,128]{1,0:T(8,128)} %height_ref.1) | copy-start | bytes 49156

commit v2 on v1

--- a/solution.py
+++ b/solution.py
@@ -17,23 +17,26 @@
 CORIOLIS_BASE = 0.3
 CORIOLIS_SLOPE = 0.4
 MESH = pl.DeviceIdType.MESH
-OFFSETS = [(dx, dy) for dx in (1, -1, 2, -2, 0) for dy in (0, 1, -1) if (dx, dy) != (0, 0)]
+STEPS = (1, -1, 2, -2)
 
 
 def step_kernel(
     gxn, gyn, mdn,
-    state_hbm, cls_ref, inv_ref, height_ref, transport_ref,
-    upd_hbm, waves_ref, corr_ref,
-    raw, mq, prov, updv, packed, from_left, from_right,
-    win, fwin, wl, fo, flow, cons, nat, mean,
-    raw_sem, out_sem, x_send, x_recv, y_send, y_recv, w_send, w_recv, f_send, f_recv,
+    state_hbm, cls_hbm, inv_hbm, height_hbm, transport_hbm,
+    upd_ref, small_ref,
+    raw, cls_ref, inv_ref, height_ref, transport_ref,
+    mq, prov, packed, from_left, from_right,
+    win, fwin, win_out, win_left, win_right, fwin_out, fwin_left, fwin_right,
+    win_side, fwin_side, wl, fo, flow, cons, nat, mean,
+    raw_sem, in_sem, x_send, x_recv, y_send, y_recv,
+    w_send, w_recv, f_send, f_recv, wy_send, wy_recv, fy_send, fy_recv,
 ):
     levels = inv_ref.shape[1]
     classes = inv_ref.shape[0]
     block = levels // classes
     rows = cls_ref.shape[0]
     cols = cls_ref.shape[1]
-    span = win.shape[2]
+    span = win.shape[1]
     strips = span // 8
     blocks = span // rows
     gx = lax.axis_index("gx")
@@ -51,21 +54,30 @@
         y2 = yy + dy
         return (gx + dx, y2 // mdn, lax.rem(y2, mdn))
 
-    offsets = [o for o in OFFSETS if abs(o[0]) < gxn and abs(o[1]) < yn]
-
+    steps = [dx for dx in STEPS if abs(dx) < gxn]
+
+    small = [
+        pltpu.make_async_copy(a, b, in_sem.at[i])
+        for i, (a, b) in enumerate((
+            (cls_hbm, cls_ref), (height_hbm, height_ref), (transport_hbm, transport_ref), (inv_hbm, inv_ref)))
+    ]
+    for c in small:
+        c.start()
     loads = [pltpu.make_async_copy(state_hbm.at[f], raw.at[f], raw_sem.at[f]) for f in range(4)]
     for c in loads:
         c.start()
 
     win[...] = jnp.zeros_like(win)
     fwin[...] = jnp.zeros_like(fwin)
+    for c in small[:3]:
+        c.wait()
     cls = cls_ref[...]
     sea = (cls > 0).astype(jnp.float32)
 
     def own(ref):
         return ref.at[:, pl.ds(pl.multiple_of(slot_of(0) * rows, rows), rows), :]
 
-    mine = own(win.at[0])
+    mine = own(win)
     mine[0] = cls.astype(jnp.float32)
     mine[1] = sea * height_ref[...]
     mine[2] = sea * transport_ref[0]
@@ -82,14 +94,18 @@
     @pl.when(yy == 0)
     def _():
         from_left[...] = jnp.zeros_like(from_left)
+        win_left[...] = jnp.zeros_like(win_left)
+        fwin_left[...] = jnp.zeros_like(fwin_left)
 
     @pl.when(yy == yn - 1)
     def _():
         from_right[...] = jnp.zeros_like(from_right)
+        win_right[...] = jnp.zeros_like(win_right)
+        fwin_right[...] = jnp.zeros_like(fwin_right)
 
     barrier = pltpu.get_barrier_semaphore()
     total = 0
-    for dx, dy in offsets:
+    for dx, dy in [(d, 0) for d in steps] + [(0, 1), (0, -1)]:
         ok = inside(dx, dy)
         total = total + ok.astype(jnp.int32)
 
@@ -149,18 +165,54 @@
             device_id=device(0, way), device_id_type=MESH)
 
     def window_copy(ref, k, send, recv, arriving):
-        dx, dy = offsets[k]
-        side = {0: 0, 1: 1, -1: 2}[dy]
+        dx = steps[k]
         if arriving:
             slot = slot_of(-dx)
         elif blocks == gxn:
             slot = gx
         else:
             slot = 2 - dx
-        dst = ref.at[side, :, pl.ds(pl.multiple_of(slot * rows, rows), rows), :]
+        dst = ref.at[:, pl.ds(pl.multiple_of(slot * rows, rows), rows), :]
         return pltpu.make_async_remote_copy(
-            src_ref=own(ref.at[0]), dst_ref=dst, send_sem=send.at[k], recv_sem=recv.at[k],
-            device_id=device(-dx, -dy) if arriving else device(dx, dy), device_id_type=MESH)
+            src_ref=own(ref), dst_ref=dst, send_sem=send.at[k], recv_sem=recv.at[k],
+            device_id=device(-dx if arriving else dx, 0), device_id_type=MESH)
+
+    def window_y_copy(out, left, right, send, recv, way):
+        i = 0 if way < 0 else 1
+        return pltpu.make_async_remote_copy(
+            src_ref=out.at[i], dst_ref=right if way < 0 else left,
+            send_sem=send.at[i], recv_sem=recv.at[i],
+            device_id=device(0, way), device_id_type=MESH)
+
+    win_y = functools.partial(window_y_copy, win_out, win_left, win_right, wy_send, wy_recv)
+    fwin_y = functools.partial(window_y_copy, fwin_out, fwin_left, fwin_right, fy_send, fy_recv)
+    wide_half = lax.broadcasted_iota(jnp.int32, (span // 2, cols), 1) < cols // 2
+
+    def pass_on(ref, out, send, recv, copy):
+        for k, dx in enumerate(steps):
+            @pl.when(inside(-dx, 0))
+            def _(k=k):
+                window_copy(ref, k, send, recv, True).wait_recv()
+
+        for j in range(ref.shape[0]):
+            top, low = ref[j, : span // 2], ref[j, span // 2 :]
+            out[0, j] = jnp.where(wide_half, top, pltpu.roll(low, cols // 2, 1))
+            out[1, j] = jnp.where(wide_half, pltpu.roll(top, cols // 2, 1), low)
+        for way in (-1, 1):
+            @pl.when(inside(0, way))
+            def _(way=way):
+                copy(way).start()
+
+    def take_sides(ref, left, right, copy, side):
+        for way in (-1, 1):
+            @pl.when(inside(0, -way))
+            def _(way=way):
+                copy(way).wait_recv()
+
+        for j in range(ref.shape[0]):
+            l, r = left[j], right[j]
+            side[j, : span // 2] = jnp.where(wide_half, r, pltpu.roll(l, cols // 2, 1))
+            side[j, span // 2 :] = jnp.where(wide_half, pltpu.roll(r, cols // 2, 1), l)
 
     for way in (-1, 1):
         @pl.when(inside(way, 0))
@@ -173,11 +225,7 @@
         def _(way=way):
             y_copy(way).start()
 
-    for k, (dx, dy) in enumerate(offsets):
-        @pl.when(inside(dx, dy))
-        def _(k=k):
-            window_copy(win, k, w_send, w_recv, False).start()
-
+    small[3].wait()
     start = 0
     for c in range(classes):
         part = inv_ref[c][: block * (c + 1), :]
@@ -245,25 +293,9 @@
         fo[0, pl.ds(x, 1), :] = jnp.sum(sum_east, axis=0, keepdims=True) * (1.0 / levels)
         fo[1, pl.ds(x, 1), :] = jnp.sum(sum_north, axis=0, keepdims=True) * (1.0 / levels)
 
-    inner_columns(tendency_column)
-    for way in (-1, 1):
-        @pl.when(inside(-way, 0))
-        def _(way=way):
-            x_copy(way).wait_recv()
-
-    edge_columns(tendency_column)
-
-    mine_f = own(fwin.at[0])
-    mine_f[0] = fo[0]
-    mine_f[1] = fo[1]
-    for k, (dx, dy) in enumerate(offsets):
-        @pl.when(inside(dx, dy))
-        def _(k=k):
-            window_copy(fwin, k, f_send, f_recv, False).start()
-
     starts = [block * c * (c + 1) // 2 for c in range(classes)]
 
-    def solve_column(x, carry):
+    def solve_column(x):
         cls_row = cls_ref[pl.ds(x, 1), :]
         for pair in (0, 2):
             p = jnp.concatenate([prov[x, pair], prov[x, pair + 1]], axis=1)
@@ -282,36 +314,60 @@
                         piece = o[r : r + block, g * cols : (g + 1) * cols]
                         picked = piece if picked is None else jnp.where(cls_row == c + 1, piece, picked)
                     where = pl.ds(x + block * b * rows, block, stride=rows)
-                    updv[f, where, :] = jnp.where(cls_row > b, picked, raw[f, where, :])
+                    upd_ref[f, where, :] = jnp.where(cls_row > b, picked, raw[f, where, :])
                     total_f = total_f + jnp.where(cls_row > b, picked, 0.0)
                 if f >= 2:
                     mean[f - 2, pl.ds(x, 1), :] = jnp.sum(total_f, axis=0, keepdims=True)
-        return carry
-
-    lax.fori_loop(0, rows, solve_column, 0)
-    stores = [pltpu.make_async_copy(updv.at[f], upd_hbm.at[f], out_sem.at[f]) for f in range(4)]
-    for c in stores:
-        c.start()
-
-    for k, (dx, dy) in enumerate(offsets):
-        @pl.when(inside(-dx, -dy))
+
+    def solve_columns(first, last):
+        def at(x, carry):
+            solve_column(x)
+            return carry
+
+        lax.fori_loop(first, last, at, 0)
+
+    inner_columns(tendency_column)
+    for way in (-1, 1):
+        @pl.when(inside(-way, 0))
+        def _(way=way):
+            x_copy(way).wait_recv()
+
+    edge_columns(tendency_column)
+
+    mine_f = own(fwin)
+    mine_f[0] = fo[0]
+    mine_f[1] = fo[1]
+    for k, dx in enumerate(steps):
+        @pl.when(inside(dx, 0))
         def _(k=k):
-            window_copy(win, k, w_send, w_recv, True).wait_recv()
-            window_copy(fwin, k, f_send, f_recv, True).wait_recv()
+            window_copy(fwin, k, f_send, f_recv, False).start()
+
+    for k, dx in enumerate(steps):
+        @pl.when(inside(dx, 0))
+        def _(k=k):
+            window_copy(win, k, w_send, w_recv, False).start()
+
+    solve_columns(0, rows // 2)
+    pass_on(fwin, fwin_out, f_send, f_recv, fwin_y)
+    pass_on(win, win_out, w_send, w_recv, win_y)
+    solve_columns(rows // 2, rows)
+    take_sides(win, win_left, win_right, win_y, win_side)
+    take_sides(fwin, fwin_left, fwin_right, fwin_y, fwin_side)
 
     half = lane < cols // 2
     place = [yy * cols + lane, yy * cols + jnp.where(half, lane + cols, lane - cols)]
     turn = [0.5 * (CORIOLIS_BASE + CORIOLIS_SLOPE * (p.astype(jnp.float32) + 0.5) / ny) for p in place]
 
-    def strip(ref, i, j):
+    def strip(refs, i, j):
         at = pl.ds(i, 8, stride=strips)
-        a = ref[0, j, at, :]
-        return a, jnp.where(half, ref[2, j, at, :], ref[1, j, at, :])
+        return refs[0][j, at, :], refs[1][j, at, :]
+
+    wins, fwins = (win, win_side), (fwin, fwin_side)
 
     for i in range(strips):
-        c = strip(win, i, 0)
-        fields = [strip(win, i, 1 + j) for j in range(3)]
-        f0, f1 = strip(fwin, i, 0), strip(fwin, i, 1)
+        c = strip(wins, i, 0)
+        fields = [strip(wins, i, 1 + j) for j in range(3)]
+        f0, f1 = strip(fwins, i, 0), strip(fwins, i, 1)
         for t in range(2):
             wet = (c[t] > 0.0).astype(jnp.float32)
             cons[0, t, i] = 0.25 * wet
@@ -364,14 +420,14 @@
             nat[j, pl.ds(i, 8, stride=strips), :] = flow[j, 0, i + 1]
     final = own(nat)
     for j in range(3):
-        waves_ref[j] = final[j]
+        small_ref[j] = final[j]
     counted = jnp.maximum(cls * block, 1).astype(jnp.float32)
     depth = jnp.maximum(cls, 1).astype(jnp.float32) * block / levels
     for j in range(2):
-        corr_ref[j] = final[1 + j] / depth - mean[j] / counted
-
-    for c in stores:
-        c.wait()
+        small_ref[3 + j] = final[1 + j] / depth - mean[j] / counted
+
+    small_ref[5] = cls.astype(jnp.float32)
+
     for way in (-1, 1):
         @pl.when(inside(way, 0))
         def _(way=way):
@@ -380,22 +436,36 @@
         @pl.when(inside(0, way))
         def _(way=way):
             y_copy(way).wait_send()
-    for k, (dx, dy) in enumerate(offsets):
-        @pl.when(inside(dx, dy))
+            win_y(way).wait_send()
+            fwin_y(way).wait_send()
+    for k, dx in enumerate(steps):
+        @pl.when(inside(dx, 0))
         def _(k=k):
             window_copy(win, k, w_send, w_recv, False).wait_send()
             window_copy(fwin, k, f_send, f_recv, False).wait_send()
 
 
-def finish_kernel(block, upd_ref, cls_ref, corr_ref, out_ref):
-    cls = cls_ref[...]
-    depth = pl.program_id(0)
+def finish_kernel(block, upd_ref, small_ref, out_hbm, height_ref, transport_ref, velocity, sem):
+    cls = small_ref[5]
     rows = cls.shape[0]
-    out_ref[0:2] = upd_ref[0:2]
-    for j in range(2):
-        add = jnp.where(cls > depth, corr_ref[j], 0.0)
-        for k in range(block):
-            out_ref[2 + j, k * rows : (k + 1) * rows] = upd_ref[2 + j, k * rows : (k + 1) * rows] + add
+    piece = block * rows
+    copies = [pltpu.make_async_copy(upd_ref.at[f], out_hbm.at[f], sem.at[f]) for f in range(2)]
+    for c in copies:
+        c.start()
+    for depth in range(upd_ref.shape[1] // piece):
+        for j in range(2):
+            add = jnp.where(cls > depth, small_ref[3 + j], 0.0)
+            for k in range(block):
+                at = slice(depth * piece + k * rows, depth * piece + (k + 1) * rows)
+                velocity[j, at] = upd_ref[2 + j, at] + add
+            at = pl.ds(depth * piece, piece)
+            copies.append(pltpu.make_async_copy(
+                velocity.at[j, at], out_hbm.at[2 + j, at], sem.at[2 + 2 * depth + j]))
+            copies[-1].start()
+    height_ref[...] = small_ref[0]
+    transport_ref[...] = small_ref[1:3]
+    for c in copies:
+        c.wait()
 
 
 def body(gxn, gyn, mdn, state, depth_class, vertical_inverse, height, transport):
@@ -406,30 +476,41 @@
     strips = span // 8
     f32 = jnp.float32
     vmem = pl.BlockSpec(memory_space=pltpu.VMEM)
-    hbm = pl.BlockSpec(memory_space=pl.ANY)
-    k = len(OFFSETS)
+    hbm = pl.BlockSpec(memory_space=pltpu.HBM)
+    k = len(STEPS)
     dma = pltpu.SemaphoreType.DMA
     wide = block * classes * (classes + 1) // 2
     flat = state.reshape(4, levels * rows, cols)
-    upd, waves, corr = pl.pallas_call(
+    keep_in_hbm = [pltpu.with_memory_space_constraint(a, pltpu.HBM) for a in (depth_class, vertical_inverse, height, transport)]
+    upd, small = pl.pallas_call(
         functools.partial(step_kernel, gxn, gyn, mdn),
         out_shape=(
             jax.ShapeDtypeStruct(flat.shape, f32),
-            jax.ShapeDtypeStruct((3, rows, cols), f32),
-            jax.ShapeDtypeStruct((2, rows, cols), f32),
+            jax.ShapeDtypeStruct((6, rows, cols), f32),
         ),
-        in_specs=[hbm, vmem, vmem, vmem, vmem],
-        out_specs=(hbm, vmem, vmem),
+        in_specs=[hbm] * 5,
+        out_specs=(vmem, vmem),
         scratch_shapes=[
             pltpu.VMEM((4, levels * rows, cols), f32),
+            pltpu.VMEM((rows, cols), jnp.int32),
+            pltpu.VMEM(vertical_inverse.shape, f32),
+            pltpu.VMEM((rows, cols), f32),
+            pltpu.VMEM((2, rows, cols), f32),
             pltpu.VMEM((4, rows + 4, levels, cols), f32),
             pltpu.VMEM((rows, 4, levels, cols), f32),
-            pltpu.VMEM((4, levels * rows, cols), f32),
             pltpu.VMEM((4, levels, cols), f32),
             pltpu.VMEM((4, levels, cols), f32),
             pltpu.VMEM((4, levels, cols), f32),
-            pltpu.VMEM((3, 4, span, cols), f32),
-            pltpu.VMEM((3, 2, span, cols), f32),
+            pltpu.VMEM((4, span, cols), f32),
+            pltpu.VMEM((2, span, cols), f32),
+            pltpu.VMEM((2, 4, span // 2, cols), f32),
+            pltpu.VMEM((4, span // 2, cols), f32),
+            pltpu.VMEM((4, span // 2, cols), f32),
+            pltpu.VMEM((2, 2, span // 2, cols), f32),
+            pltpu.VMEM((2, span // 2, cols), f32),
+            pltpu.VMEM((2, span // 2, cols), f32),
+            pltpu.VMEM((4, span, cols), f32),
+            pltpu.VMEM((2, span, cols), f32),
             pltpu.VMEM((wide, 3 * levels), jnp.bfloat16),
             pltpu.VMEM((2, rows, cols), f32),
             pltpu.VMEM((3, 2, strips + 2, 8, cols), f32),
@@ -437,26 +518,26 @@
             pltpu.VMEM((3, span, cols), f32),
             pltpu.VMEM((2, rows, cols), f32),
             dma((4,)), dma((4,)), dma((2,)), dma((2,)), dma((2,)), dma((2,)),
-            dma((k,)), dma((k,)), dma((k,)), dma((k,)),
+            dma((k,)), dma((k,)), dma((k,)), dma((k,)), dma((2,)), dma((2,)), dma((2,)), dma((2,)),
         ],
         compiler_params=pltpu.CompilerParams(
             collective_id=0, has_side_effects=True, vmem_limit_bytes=48 * 2**20),
         cost_estimate=pl.CostEstimate(flops=10**9, bytes_accessed=2**23, transcendentals=0),
-    )(flat, depth_class, vertical_inverse, height, transport)
-    out = pl.pallas_call(
+    )(flat, *keep_in_hbm)
+    out, height_next, transport_next = pl.pallas_call(
         functools.partial(finish_kernel, block),
-        grid=(classes,),
-        out_shape=jax.ShapeDtypeStruct(flat.shape, f32),
-        in_specs=[
-            pl.BlockSpec((4, block * rows, cols), lambda i: (0, i, 0)),
-            pl.BlockSpec((rows, cols), lambda i: (0, 0)),
-            pl.BlockSpec((2, rows, cols), lambda i: (0, 0, 0)),
-        ],
-        out_specs=pl.BlockSpec((4, block * rows, cols), lambda i: (0, i, 0)),
+        out_shape=(
+            jax.ShapeDtypeStruct(flat.shape, f32),
+            jax.ShapeDtypeStruct((rows, cols), f32),
+            jax.ShapeDtypeStruct((2, rows, cols), f32),
+        ),
+        in_specs=[vmem, vmem],
+        out_specs=(pl.BlockSpec(memory_space=pl.ANY), vmem, vmem),
+        scratch_shapes=[pltpu.VMEM((2, levels * rows, cols), f32), dma((2 + 2 * classes,))],
         compiler_params=pltpu.CompilerParams(vmem_limit_bytes=24 * 2**20),
         cost_estimate=pl.CostEstimate(flops=2**20, bytes_accessed=2**23, transcendentals=0),
-    )(upd, depth_class, corr)
-    return out.reshape(state.shape), waves[0], waves[1:3]
+    )(upd, small)
+    return out.reshape(state.shape), height_next, transport_next
 
 
 def solution(mesh):

time: 54.7 us -> 50.1 us (0.916)
  local copies, waits for them, and re-layouts: 4.31 us -> 0 us
    unnamed x8 -> x0, local copies, waits for them, and re-layouts: 3.09 us -> none
    slice x1 -> x0, local copies, waits for them, and re-layouts: 0.62 us -> none  [body(): return (out.reshape(state.shape), waves[0], waves[1:3])]
    squeeze x1 -> x0, local copies, waits for them, and re-layouts: 0.61 us -> none  [body(): return (out.reshape(state.shape), waves[0], waves[1:3])]
where the time goes in v2:
time: 50.1 us; the launch traced here: 49.8 us
  Pallas kernels  49.2 us (98%)
  between operations  0.64 us (1%)
    pallas_call x1, Pallas kernels, body(): pl.pallas_call(functools.partial(step_kernel, gxn, gyn, mdn), out_shape=(...  46.5 us
    pallas_call x1, Pallas kernels, body(): pl.pallas_call(functools.partial(finish_kernel, block), out_shape=(jax.Sh...  2.7 us

profile of v2, /device:TPU:1, one launch (start us, length us, event | category | flops | bytes accessed | tf_op | source)
XLA Modules:
  0.0 49.8 jit_solution(6392969904149576509)
XLA Ops:
  0.6 46.5 %shard_map.76 = (f32[4,2048,128]{2,1,0:T(8,128)S(1)}, f32[6,32,128]{2,1,0:T(8,128)S(1)}) custom-call(f32[4,2048,128]{2,1,0:T(8,128)} %bitcast.2, s32[32,128]{1,0:T(8,128)} %cls_hbm.1, f32[4,64,64]{2,1,0:T(8,128)} %inv_hbm.1, f32[32,128]{1,0:T(8,128)} %height_hbm.1, f32[2,32,128]{2,1,0:T(8,128)} %transport_hbm.1), custom_call_target="tpu_custom_call" | custom-call | flops 1000000000 | bytes 8388608 | tf_op jit(solution)/shard_map/pallas_call | solution.py:485
  47.1 2.7 %shard_map.77 = (f32[4,2048,128]{2,1,0:T(8,128)}, f32[32,128]{1,0:T(8,128)}, f32[2,32,128]{2,1,0:T(8,128)}) custom-call(f32[4,2048,128]{2,1,0:T(8,128)S(1)} %get-tuple-element.8.upd_ref, f32[6,32,128]{2,1,0:T(8,128)S(1)} %get-tuple-element.9.small_ref), custom_call_target="tpu_custom_call" | custom-call | flops 1048576 | bytes 8388608 | tf_op jit(solution)/shard_map/pallas_call | solution.py:527

commit v3 on v2

--- a/solution.py
+++ b/solution.py
@@ -118,20 +118,30 @@
         c.wait()
 
     level_block = lax.broadcasted_iota(jnp.int32, (levels, cols), 0) // block
-    lane_full = lax.broadcasted_iota(jnp.int32, (levels, cols), 1)
     lane = lax.broadcasted_iota(jnp.int32, (8, cols), 1)
     sub = lax.broadcasted_iota(jnp.int32, (8, cols), 0)
 
     def mask_column(x):
         act = level_block < cls_ref[pl.ds(x, 1), :]
-        spot = (lane_full >= 4 * x) & (lane_full < 4 * x + 4)
-        shift = lax.rem(4 * x + 2, cols)
         for f in range(4):
             v = jnp.where(act, raw[f, pl.ds(x, levels, stride=rows), :], 0.0)
             mq[f, x + 2] = v
-            packed[f] = jnp.where(spot, pltpu.roll(v, shift, 1), packed[f])
-
-    packed[...] = jnp.zeros_like(packed)
+
+    def mask_levels(chunk, carry):
+        depth = chunk // (block // 8)
+        for f in range(4):
+            lanes = jnp.zeros((8, cols), jnp.float32)
+            for x in range(rows):
+                v = raw[f, pl.ds(chunk * (8 * rows) + x, 8, stride=rows), :]
+                v = jnp.where(cls_ref[x : x + 1, :] > depth, v, 0.0)
+                at = pl.ds(pl.multiple_of(chunk * 8, 8), 8)
+                if 2 <= x < rows - 2:
+                    mq[f, x + 2, at, :] = v
+                spot = (lane >= 4 * x) & (lane < 4 * x + 4)
+                lanes = jnp.where(spot, pltpu.roll(v, (4 * x + 2) % cols, 1), lanes)
+            packed[f, at, :] = lanes
+        return carry
+
 
     def edge_columns(work):
         def at(e, carry):
@@ -219,7 +229,7 @@
         def _(way=way):
             x_copy(way).start()
 
-    inner_columns(mask_column)
+    lax.fori_loop(0, levels // 8, mask_levels, 0)
     for way in (-1, 1):
         @pl.when(inside(0, way))
         def _(way=way):
@@ -324,7 +334,7 @@
             solve_column(x)
             return carry
 
-        lax.fori_loop(first, last, at, 0)
+        lax.fori_loop(first, last, at, 0, unroll=2)
 
     inner_columns(tendency_column)
     for way in (-1, 1):

time: 50.1 us -> 45.6 us (0.910)
  Pallas kernels: 49.2 us -> 44.5 us
    pallas_call x1, Pallas kernels: 46.5 us -> 41.8 us  [body(): pl.pallas_call(functools.partial(step_kernel, gxn, gyn, mdn), out_shape=(...]
where the time goes in v3:
time: 45.6 us; the launch traced here: 45.1 us
  Pallas kernels  44.5 us (98%)
  between operations  0.64 us (1%)
    pallas_call x1, Pallas kernels, body(): pl.pallas_call(functools.partial(step_kernel, gxn, gyn, mdn), out_shape=(...  41.8 us
    pallas_call x1, Pallas kernels, body(): pl.pallas_call(functools.partial(finish_kernel, block), out_shape=(jax.Sh...  2.7 us

profile of v3, /device:TPU:1, one launch (start us, length us, event | category | flops | bytes accessed | tf_op | source)
XLA Modules:
  0.0 45.1 jit_solution(640696789281523636)
XLA Ops:
  0.6 41.8 %shard_map.76 = (f32[4,2048,128]{2,1,0:T(8,128)S(1)}, f32[6,32,128]{2,1,0:T(8,128)S(1)}) custom-call(f32[4,2048,128]{2,1,0:T(8,128)} %bitcast.2, s32[32,128]{1,0:T(8,128)} %cls_hbm.1, f32[4,64,64]{2,1,0:T(8,128)} %inv_hbm.1, f32[32,128]{1,0:T(8,128)} %height_hbm.1, f32[2,32,128]{2,1,0:T(8,128)} %transport_hbm.1), custom_call_target="tpu_custom_call" | custom-call | flops 1000000000 | bytes 8388608 | tf_op jit(solution)/shard_map/pallas_call | solution.py:495
  42.4 2.7 %shard_map.77 = (f32[4,2048,128]{2,1,0:T(8,128)}, f32[32,128]{1,0:T(8,128)}, f32[2,32,128]{2,1,0:T(8,128)}) custom-call(f32[4,2048,128]{2,1,0:T(8,128)S(1)} %get-tuple-element.8.upd_ref, f32[6,32,128]{2,1,0:T(8,128)S(1)} %get-tuple-element.9.small_ref), custom_call_target="tpu_custom_call" | custom-call | flops 1048576 | bytes 8388608 | tf_op jit(solution)/shard_map/pallas_call | solution.py:537
